TPU v7x, 128 devices: a whole 4x4x4 slice. The times are simulated.
128 devices in a mesh: comp: 2 (over z_lo), tx: 8 (over z_hi, x), ty: 8 (over y, core).
Axes of the slice: x: 4, y: 4, z: 4 (z_hi: 2, z_lo: 2; z = z_hi * 2 + z_lo), core: 2. Of those that a mesh axis runs over, the one named last changes fastest.
Arguments:
- state: float32 [2, 16, 1024, 4096], P('comp', None, 'tx', 'ty'), may hold values from -6 to 6
- coefs: float32 [2, 3, 1024, 4096], P('comp', None, 'tx', 'ty'), may hold values from -0.2 to 0.2
- land_sea: int32 [1024, 4096], P('tx', 'ty'), may hold values 0 or 1
- gamma: float32 [2, 8], P('comp'), may hold values from 0.1 to 0.4
- pair_src: int32 [2, 32768], P('comp', ('tx', 'ty')), may hold values from 0 to 511
- pair_dev: int32 [2, 32768, 1], P('comp', ('tx', 'ty')), may hold values from 0 to 63; in each aligned block of 512 rows (0 to 511, 512 to 1023, ..., all dimensions but the last counted through in order) at most 16 rows name the same one
- pair_blk: int32 [2, 32768], P('comp', ('tx', 'ty')), may hold values from 0 to 511
- weights: bfloat16 [2, 32768, 128, 128], P('comp', ('tx', 'ty')), may hold values from -0.375 to 0.375
Outputs:
- new_state: float32 [2, 16, 1024, 4096], P('comp', None, 'tx', 'ty')
- remapped: float32 [2, 8, 1024, 4096], P('comp', None, 'tx', 'ty')
Inputs may be any that keep to these rules, and one draw needn't show every extreme that they name: `pair_dev`: among the 512 weight blocks of one tile of one component, at most 16 name the same target tile, a bound that some block reaches.
All inputs are finite; a program needn't handle non-finite values. No bound on the sum of `land_sea` on one device may be relied on, other than what follows from the above.
Results may differ from a plain program's by a relative error of at most 0.0029.
Values sent between devices are 32-bit elements; how exact they have to be, the bound alone decides.
A program may use at most 128 MiB of HBM per device.

v0:
```python
import jax
import jax.numpy as jnp
from jax import lax
from jax.sharding import PartitionSpec as P


def swapped(block, axis, bit):
    count = lax.axis_size(axis)
    route = []
    for low in range(count):
        high = low | 1 << bit
        if high != low and high < count:
            route += [(low, high), (high, low)]
    return lax.ppermute(block, axis, route)


def extended(cells, sides, width):
    for axis, dim in sides:
        count = lax.axis_size(axis)
        ends = count - 1
        head = lax.slice_in_dim(cells, 0, width, axis=dim)
        tail = lax.slice_in_dim(cells, cells.shape[dim] - width, cells.shape[dim], axis=dim)
        cells = jnp.concatenate(
            [
                lax.ppermute(tail, axis, [(i, (i + 1) % count) for i in range(ends)]),
                cells,
                lax.ppermute(head, axis, [((i + 1) % count, i) for i in range(ends)]),
            ],
            axis=dim,
        )
    return cells


def tendency(padded, coefs, recv, gamma, keep):
    center = padded[:, 1:-1, 1:-1]
    xminus = padded[:, :-2, 1:-1]
    xplus = padded[:, 2:, 1:-1]
    yminus = padded[:, 1:-1, :-2]
    yplus = padded[:, 1:-1, 2:]
    speed_x = coefs[0]
    speed_y = coefs[1]
    kappa = coefs[2]
    advect = -(
        jnp.maximum(speed_x, 0.0) * (center - xminus) + jnp.minimum(speed_x, 0.0) * (xplus - center)
    )
    advect = advect - (
        jnp.maximum(speed_y, 0.0) * (center - yminus) + jnp.minimum(speed_y, 0.0) * (yplus - center)
    )
    diffuse = kappa * (xplus + xminus + yplus + yminus - 4.0 * center)
    chan = recv.shape[0]
    couple = gamma[:, None, None] * (recv - center[:chan])
    couple = jnp.concatenate([couple, jnp.zeros_like(center[chan:])], axis=0)
    return keep * (advect + diffuse + couple)


def partner(buffers):
    return swapped((buffers[0], buffers[1]), "comp", 0)


def shallow_rims(field):
    return extended(field, (("tx", 1), ("ty", 2)), 1)


def body(state, coefs, land_sea, gamma, pair_src, pair_dev, pair_blk, weights):
    comp_index = lax.axis_index("comp")
    rows_tx = lax.axis_size("tx")
    rows_ty = lax.axis_size("ty")
    tiles = rows_tx * rows_ty
    nfield, cells_x, cells_y = (state.shape[1], state.shape[2], state.shape[3])
    chan = gamma.shape[1]
    pairs = weights.shape[1]
    width = weights.shape[2]
    nblock = cells_x * cells_y // width
    capacity = max(2, 2 * pairs // tiles)
    surface = state[0, :chan].reshape(chan, nblock, width).astype(jnp.bfloat16)
    picked = jnp.take(surface, pair_src[0], axis=1)
    contrib = jnp.einsum("pts,cps->pct", weights[0], picked, preferred_element_type=jnp.float32)
    target_tile = pair_dev[0, :, 0]
    member = (target_tile[:, None] == jnp.arange(tiles, dtype=jnp.int32)[None, :]).astype(jnp.int32)
    rank = jnp.sum(jnp.cumsum(member, axis=0) * member, axis=1) - 1
    slot = target_tile * capacity + rank
    outgoing = jnp.zeros((tiles * capacity, chan, width), jnp.float32).at[slot].set(contrib)
    out_ids = jnp.zeros((tiles * capacity,), jnp.int32).at[slot].set(pair_blk[0])
    outgoing, out_ids = partner((outgoing, out_ids))
    incoming, in_ids = (
        lax.all_to_all(
            outgoing.reshape(tiles, capacity, chan, width),
            ("tx", "ty"),
            split_axis=0,
            concat_axis=0,
            tiled=True,
        ),
        lax.all_to_all(
            out_ids.reshape(tiles, capacity), ("tx", "ty"), split_axis=0, concat_axis=0, tiled=True
        ),
    )
    incoming = incoming.reshape(tiles * capacity, chan, width)
    in_ids = in_ids.reshape(tiles * capacity)
    selector = (in_ids[:, None] == jnp.arange(nblock, dtype=jnp.int32)[None, :]).astype(jnp.float32)
    summed = jnp.einsum("sn,scb->cnb", selector, incoming, precision=lax.Precision.HIGHEST)
    recv = summed.reshape(chan, cells_x, cells_y)
    is_atmos = comp_index == 0
    keep = jnp.where(
        is_atmos, jnp.ones((cells_x, cells_y), jnp.float32), land_sea.astype(jnp.float32)
    )
    mix_a = jnp.where(is_atmos, 0.0, 0.5).astype(jnp.float32)
    mix_b = jnp.where(is_atmos, 1.0, 0.5).astype(jnp.float32)
    start = state[0]
    local_coefs = coefs[0]
    rates = gamma[0]
    first = tendency(shallow_rims(start), local_coefs, recv, rates, keep)
    section = start + first
    second = tendency(shallow_rims(section), local_coefs, recv, rates, keep)
    result = mix_a * start + (1.0 - mix_a) * section + mix_b * second
    return (result[None], recv[None])


def solution(mesh):
    placed = (
        P("comp", None, "tx", "ty"),
        P("comp", None, "tx", "ty"),
        P("tx", "ty"),
        P("comp", None),
        P("comp", ("tx", "ty")),
        P("comp", ("tx", "ty"), None),
        P("comp", ("tx", "ty")),
        P("comp", ("tx", "ty"), None, None),
    )
    return jax.shard_map(
        body,
        mesh=mesh,
        in_specs=placed,
        out_specs=(P("comp", None, "tx", "ty"), P("comp", None, "tx", "ty")),
        check_vma=False,
    )
```

profile of v0, /device:TPU:9, one launch (start us, length us, event | category | flops | bytes accessed | tf_op | source)
XLA Modules:
  0.0 333.3 jit_solution(10902521976681935122)
XLA Ops:
  0.6 0.7 compare_select_fusion
  1.3 0.7 compare_and_fusion
  2.0 0.7 fusion.54
  2.7 1.2 reduce-window.6
  3.9 0.2 slice_reduce_fusion
  4.2 0.8 fusion.53
  5.0 0.7 compare_select_fusion.1
  5.7 1.7 slice.130
  7.4 0.7 convert_element_type.18
  8.1 0.7 copy.24
  8.8 1.8 gather_fusion
  10.6 11.8 %fusion = f32[512,8,128]{2,1,0:T(8,128)S(1)} fusion(bf16[1,512,128,128]{3,2,1,0:T(8,128)(2,1)} %param.15, bf16[512,8,128]{2,1,0:T(8,128)(2,1)S(1)} %gather_fusion, pred[512]{0:T(512)(128)(4,1)S(1)} %compare_and_fusion), kind=kOutput, calls=%fused_computation.3 | convolution fusion | flops 134742016 | bytes 19923456 | tf_op jit(solution)/shard_map/pts,cps->pct/dot_general | solution.py:77
  22.4 2.3 broadcast_in_dim.19
  24.7 50.5 %scatter_fusion = f32[1024,8,128]{2,1,0:T(8,128)} fusion(f32[1024,8,128]{2,1,0:T(8,128)} %broadcast_in_dim.19, s32[512]{0:T(512)S(1)} %bitcast.73, f32[512,8,128]{2,1,0:T(8,128)S(1)} %fusion), kind=kCustom, calls=%fused_computation.1 | custom fusion | bytes 6293504 | tf_op jit(solution)/shard_map/scatter | solution.py:82
  75.2 1.6 collective-permute-start.4
  76.8 2.6 scatter_custom_fusion.1
  79.4 0.1 collective-permute-start.5
  79.5 87.9 %collective-permute-done.5 = s32[1024]{0:T(1024)S(1)} collective-permute-done((s32[1024]{0:T(1024)S(1)}, s32[1024]{0:T(1024)S(1)}, u32[]{:S(2)}, u32[]{:S(2)}) %collective-permute-start.5) | collective-permute-done | bytes 4128 | tf_op jit(solution)/shard_map/ppermute | solution.py:14
  167.4 0.1 all_to_all.10
  167.5 20.1 %all_to_all.14 = s32[64,1,16]{2,1,0:T(1,128)S(1)} all-to-all(s32[64,1,16]{2,1,0:T(1,128)S(1)} %bitcast.70), channel_id=1, replica_groups=mesh['comp'=2,'tx'=8,'ty'=8] {'tx','ty'}, dimensions={0} | all-to-all | bytes 8192 | tf_op jit(solution)/shard_map/all_to_all | solution.py:93
  187.5 6.9 %all-to-all-start = ((f32[64,16,8,128]{3,2,1,0:T(8,128)}), f32[64,16,8,128]{3,2,1,0:T(8,128)}, u32[]{:S(2)}, u32[]{:S(2)}) async-start(f32[64,16,8,128]{3,2,1,0:T(8,128)} %bitcast.18), calls=%async_computation | async-start | bytes 8388608 | tf_op jit(solution)/shard_map/all_to_all | solution.py:86
  194.5 1.1 fusion.59
  195.6 3.1 collective-permute-start
  198.7 1.3 collective-permute-start.1
  200.0 1.1 maximum_bitcast_fusion.1
  201.1 41.6 %collective-permute-done = f32[16,1,512]{2,1,0:T(1,128)S(1)} collective-permute-done((f32[16,1,512]{2,1,0:T(1,128)S(1)}, f32[16,1,512]{2,1,0:T(1,128)S(1)}, u32[]{:S(2)}, u32[]{:S(2)}) %collective-permute-start) | collective-permute-done | bytes 32800 | tf_op jit(solution)/shard_map/ppermute | solution.py:25
  242.7 0.2 collective-permute-done.1
  242.9 2.0 pad_maximum_fusion.21
  244.9 0.6 copy.19
  245.5 0.6 copy.21
  246.1 2.7 collective-permute-start.3
  248.8 4.3 %collective-permute-start.2 = (f32[16,130,1]{1,0,2:T(8,128)S(1)}, f32[16,130,1]{1,0,2:T(8,128)S(1)}, u32[]{:S(2)}, u32[]{:S(2)}) collective-permute-start(f32[16,130,1]{1,0,2:T(8,128)S(1)} %copy.19), channel_id=1, source_target_pairs={{0,1},{1,2},{2,3},{3,4},{4,5},{5,6},{6,7},{8,9},{9,10},{10,11},{11... | collective-permute-start | bytes 24968 | tf_op jit(solution)/shard_map/ppermute | solution.py:25
  253.2 0.5 broadcast.154
  253.7 0.7 reduce.5
  254.4 0.1 eq.52
  254.5 0.3 collective-permute-done.2
  254.8 0.4 copy.20
  255.2 1.4 copy.22
  256.7 6.1 %fusion.42 = f32[8,512,128]{1,2,0:T(8,128)S(1)} fusion(f32[1024,8,128]{2,1,0:T(8,128)} %bitcast.19, s32[1024]{0:T(1024)S(1)} %eq.52), kind=kOutput, calls=%fused_computation.64 | convolution fusion | flops 6442975232 | bytes 6295552 | tf_op jit(solution)/shard_map/sn,scb->cnb/dot_general | solution.py:100
  262.8 1.8 copy.27
  264.6 1.7 reshape.144
  266.3 0.0 copy-start
  266.4 2.4 fusion.39
  268.8 0.4 copy-done
  269.2 0.3 copy-done.3
  269.5 0.0 copy-done.4
  269.5 0.1 copy-done.5
  269.6 0.1 copy-done.6
  269.7 10.0 %fusion.29 = f32[16,128,512]{2,1,0:T(8,128)S(1)} fusion(f32[16,128,512]{2,1,0:T(8,128)S(1)} %bitcast.69, f32[16,1,512]{2,1,0:T(1,128)S(1)} %collective-permute-done.1, f32[16,1,512]{2,1,0:T(1,128)S(1)} %collective-permute-done, f32[8,128,512]{2,1,0:T(8,128)S(1)} %fusion.39, f32[16,130,1]{2,1,0:T(8,128)S(1)} %copy-done.3, f32[16,130,1]{2,1,0:T(8,128)S(1)} %copy.20, ...), kind=kLoop, calls=%fused_computation.47 | loop fusion | flops 31457280 | bytes 12140800 | tf_op jit(solution)/shard_map/add | solution.py:112
  279.7 1.9 copy-done.1
  281.6 0.1 fusion.58
  281.7 3.8 %collective-permute-start.6 = (f32[16,1,512]{2,1,0:T(1,128)S(1)}, f32[16,1,512]{2,1,0:T(1,128)S(1)}, u32[]{:S(2)}, u32[]{:S(2)}) collective-permute-start(f32[16,1,512]{2,1,0:T(1,128)S(1)} %get-tuple-element.6), channel_id=1, source_target_pairs={{0,8},{8,16},{16,24},{24,32},{32,40},{40,48},{48,56},{1,9},{9,17},... | collective-permute-start | bytes 98312 | tf_op jit(solution)/shard_map/ppermute | solution.py:25
  285.5 1.3 collective-permute-start.7
  286.8 7.0 %collective-permute-done.7 = f32[16,1,512]{2,1,0:T(1,128)S(1)} collective-permute-done((f32[16,1,512]{2,1,0:T(1,128)S(1)}, f32[16,1,512]{2,1,0:T(1,128)S(1)}, u32[]{:S(2)}, u32[]{:S(2)}) %collective-permute-start.7) | collective-permute-done | bytes 32800 | tf_op jit(solution)/shard_map/ppermute | solution.py:27
  293.8 3.0 pad_maximum_fusion.18
  296.8 2.4 copy.28
  299.2 0.6 copy.30
  299.8 5.5 %collective-permute-start.9 = (f32[16,130,1]{1,0,2:T(8,128)S(1)}, f32[16,130,1]{1,0,2:T(8,128)}, u32[]{:S(2)}, u32[]{:S(2)}) collective-permute-start(f32[16,130,1]{1,0,2:T(8,128)S(1)} %copy.30), channel_id=1, source_target_pairs={{1,0},{2,1},{3,2},{4,3},{5,4},{6,5},{7,6},{9,8},{10,9},{11,10},{12... | collective-permute-start | bytes 24968 | tf_op jit(solution)/shard_map/ppermute | solution.py:27
  305.4 2.1 collective-permute-start.8
  307.5 3.5 %fusion.38 = f32[8,128,512]{2,1,0:T(8,128)} fusion(f32[8,128,512]{2,1,0:T(8,128)S(1)} %reshape.144, f32[16,128,512]{2,1,0:T(8,128)} %copy-done.1, f32[8]{0:T(128)} %bitcast.78), kind=kLoop, calls=%fused_computation.58 | loop fusion | flops 1048576 | bytes 6291488 | tf_op jit(solution)/shard_map/mul | solution.py:51
  311.1 2.9 broadcast_in_dim_reshape.4
  313.9 1.1 copy.29
  315.1 2.2 copy.31
  317.2 16.1 %fusion.13 = f32[1,16,128,512]{3,2,1,0:T(8,128)} fusion(f32[16,1,512]{2,1,0:T(1,128)S(1)} %collective-permute-done.7, f32[16,128,512]{2,1,0:T(8,128)} %copy-done.1, f32[16,1,512]{2,1,0:T(1,128)S(1)} %collective-permute-done.6, f32[8,128,512]{2,1,0:T(8,128)S(1)} %copy-done.2, f32[16,130,1]{2,1,0:T(8,128)} %copy.31, f32[16,130,1]{2,1,0:T(8,128)S(1)} %copy.29, ...), kind=kLoop, calls=%fused_computation.23 | loop fusion | flops 35651584 | bytes 16335116 | tf_op jit(solution)/shard_map/broadcast_in_dim | solution.py:115
  (24 shorter events, 0.1 us)
Async XLA Ops:
  75.2 112.4 %collective-permute-start.4 = (f32[1024,8,128]{2,1,0:T(8,128)}, f32[1024,8,128]{2,1,0:T(8,128)}, u32[]{:S(2)}, u32[]{:S(2)}) collective-permute-start(f32[1024,8,128]{2,1,0:T(8,128)} %scatter_fusion), channel_id=1, source_target_pairs={{0,64},{64,0},{1,65},{65,1},{2,66},{66,2},{3,67},{67,3},{4,68},{68... | collective-permute-start | bytes 12582920 | tf_op jit(solution)/shard_map/ppermute | solution.py:14
  79.4 88.0 %collective-permute-start.5 = (s32[1024]{0:T(1024)S(1)}, s32[1024]{0:T(1024)S(1)}, u32[]{:S(2)}, u32[]{:S(2)}) collective-permute-start(s32[1024]{0:T(1024)S(1)} %scatter_custom_fusion.1), channel_id=1, source_target_pairs={{0,64},{64,0},{1,65},{65,1},{2,66},{66,2},{3,67},{67,3},{4,68},{68... | collective-permute-start | bytes 12296 | tf_op jit(solution)/shard_map/ppermute | solution.py:14
  187.5 12.5 %copy-start.7 = (f32[1,3,128,512]{3,2,1,0:T(8,128)S(1)}, f32[1,3,128,512]{3,2,1,0:T(8,128)}, u32[]{:S(2)}) copy-start(f32[1,3,128,512]{3,2,1,0:T(8,128)} %param.9) | copy-start | bytes 2359300
  187.5 69.1 %all-to-all-start = ((f32[64,16,8,128]{3,2,1,0:T(8,128)}), f32[64,16,8,128]{3,2,1,0:T(8,128)}, u32[]{:S(2)}, u32[]{:S(2)}) async-start(f32[64,16,8,128]{3,2,1,0:T(8,128)} %bitcast.18), calls=%async_computation | async-start | bytes 8388608 | tf_op jit(solution)/shard_map/all_to_all | solution.py:86
  195.6 47.2 %collective-permute-start = (f32[16,1,512]{2,1,0:T(1,128)S(1)}, f32[16,1,512]{2,1,0:T(1,128)S(1)}, u32[]{:S(2)}, u32[]{:S(2)}) collective-permute-start(f32[16,1,512]{2,1,0:T(1,128)S(1)} %get-tuple-element.8), channel_id=1, source_target_pairs={{0,8},{8,16},{16,24},{24,32},{32,40},{40,48},{48,56},{1,9},{9,17},... | collective-permute-start | bytes 98312 | tf_op jit(solution)/shard_map/ppermute | solution.py:25
  198.7 44.2 %collective-permute-start.1 = (f32[16,1,512]{2,1,0:T(1,128)S(1)}, f32[16,1,512]{2,1,0:T(1,128)S(1)}, u32[]{:S(2)}, u32[]{:S(2)}) collective-permute-start(f32[16,1,512]{2,1,0:T(1,128)S(1)} %get-tuple-element.9), channel_id=1, source_target_pairs={{8,0},{16,8},{24,16},{32,24},{40,32},{48,40},{56,48},{9,1},{17,9},... | collective-permute-start | bytes 98312 | tf_op jit(solution)/shard_map/ppermute | solution.py:27
  201.1 52.0 %copy-start.8 = (s32[128,512]{1,0:T(8,128)S(1)}, s32[128,512]{1,0:T(8,128)}, u32[]{:S(2)}) copy-start(s32[128,512]{1,0:T(8,128)} %param.10) | copy-start | bytes 786436
  246.1 9.1 %collective-permute-start.3 = (f32[16,130,1]{1,0,2:T(8,128)S(1)}, f32[16,130,1]{1,0,2:T(8,128)S(1)}, u32[]{:S(2)}, u32[]{:S(2)}) collective-permute-start(f32[16,130,1]{1,0,2:T(8,128)S(1)} %copy.21), channel_id=1, source_target_pairs={{1,0},{2,1},{3,2},{4,3},{5,4},{6,5},{7,6},{9,8},{10,9},{11,10},{12... | collective-permute-start | bytes 24968 | tf_op jit(solution)/shard_map/ppermute | solution.py:27
  248.8 6.0 %collective-permute-start.2 = (f32[16,130,1]{1,0,2:T(8,128)S(1)}, f32[16,130,1]{1,0,2:T(8,128)S(1)}, u32[]{:S(2)}, u32[]{:S(2)}) collective-permute-start(f32[16,130,1]{1,0,2:T(8,128)S(1)} %copy.19), channel_id=1, source_target_pairs={{0,1},{1,2},{2,3},{3,4},{4,5},{5,6},{6,7},{8,9},{9,10},{10,11},{11... | collective-permute-start | bytes 24968 | tf_op jit(solution)/shard_map/ppermute | solution.py:25
  262.8 3.6 %copy-start.9 = (f32[1,8]{1,0:T(1,128)S(1)}, f32[1,8]{1,0:T(1,128)}, u32[]{:S(2)}) copy-start(f32[1,8]{1,0:T(1,128)} %param.11) | copy-start | bytes 100
  266.3 2.8 copy-start
  266.3 3.1 copy-start.3
  266.4 3.1 copy-start.4
  266.4 3.2 copy-start.5
  266.4 3.3 copy-start.6
  279.7 1.9 copy-start.1
  281.7 5.1 %collective-permute-start.6 = (f32[16,1,512]{2,1,0:T(1,128)S(1)}, f32[16,1,512]{2,1,0:T(1,128)S(1)}, u32[]{:S(2)}, u32[]{:S(2)}) collective-permute-start(f32[16,1,512]{2,1,0:T(1,128)S(1)} %get-tuple-element.6), channel_id=1, source_target_pairs={{0,8},{8,16},{16,24},{24,32},{32,40},{40,48},{48,56},{1,9},{9,17},... | collective-permute-start | bytes 98312 | tf_op jit(solution)/shard_map/ppermute | solution.py:25
  285.5 8.3 %collective-permute-start.7 = (f32[16,1,512]{2,1,0:T(1,128)S(1)}, f32[16,1,512]{2,1,0:T(1,128)S(1)}, u32[]{:S(2)}, u32[]{:S(2)}) collective-permute-start(f32[16,1,512]{2,1,0:T(1,128)S(1)} %get-tuple-element.7), channel_id=1, source_target_pairs={{8,0},{16,8},{24,16},{32,24},{40,32},{48,40},{56,48},{9,1},{17,9},... | collective-permute-start | bytes 98312 | tf_op jit(solution)/shard_map/ppermute | solution.py:27
  299.8 15.2 %collective-permute-start.9 = (f32[16,130,1]{1,0,2:T(8,128)S(1)}, f32[16,130,1]{1,0,2:T(8,128)}, u32[]{:S(2)}, u32[]{:S(2)}) collective-permute-start(f32[16,130,1]{1,0,2:T(8,128)S(1)} %copy.30), channel_id=1, source_target_pairs={{1,0},{2,1},{3,2},{4,3},{5,4},{6,5},{7,6},{9,8},{10,9},{11,10},{12... | collective-permute-start | bytes 24968 | tf_op jit(solution)/shard_map/ppermute | solution.py:27
  305.4 8.5 %collective-permute-start.8 = (f32[16,130,1]{1,0,2:T(8,128)}, f32[16,130,1]{1,0,2:T(8,128)}, u32[]{:S(2)}, u32[]{:S(2)}) collective-permute-start(f32[16,130,1]{1,0,2:T(8,128)} %copy.28), channel_id=1, source_target_pairs={{0,1},{1,2},{2,3},{3,4},{4,5},{5,6},{6,7},{8,9},{9,10},{10,11},{11... | collective-permute-start | bytes 24968 | tf_op jit(solution)/shard_map/ppermute | solution.py:25
  311.1 6.2 %copy-start.2 = (f32[8,128,512]{2,1,0:T(8,128)S(1)}, f32[8,128,512]{2,1,0:T(8,128)}, u32[]{:S(2)}) copy-start(f32[8,128,512]{2,1,0:T(8,128)} %fusion.38) | copy-start | bytes 6291460
where the time goes:
time: 338 us; the launch traced here: 333 us
  waiting for transfers between devices  137 us (41%)
  local copies, waits for them, and re-layouts  81 us (24%)
  other arithmetic  43.6 us (13%)
  starting transfers between devices  32.9 us (10%)
  blocking collectives  20.1 us (6%)
  matrix products  17.9 us (5%)
    ppermute x2, waiting for transfers between devices, swapped(): return lax.ppermute(block, axis, route)  87.9 us
    scatter x1, local copies, waits for them, and re-layouts, body(): jnp.zeros((tiles * capacity, chan, width), jnp.float32).at[slot]  50.5 us
    ppermute x4, waiting for transfers between devices, extended(): lax.ppermute(tail, axis, [(i, (i + 1) % count) for i in range(ends)])  41.8 us
    all_to_all x1, blocking collectives, body(): lax.all_to_all(out_ids.reshape(tiles, capacity), ('tx', 'ty'), split_axis...  20.1 us
    broadcast_in_dim x1, other arithmetic, body(): return (result[None], recv[None])  16.1 us
    ppermute x4, starting transfers between devices, extended(): lax.ppermute(tail, axis, [(i, (i + 1) % count) for i in range(ends)])  13.5 us
    dot_general x1, matrix products, body(): jnp.einsum('pts,cps->pct', weights[0], picked, preferred_element_type=jnp...  11.8 us
    ppermute x4, starting transfers between devices, extended(): lax.ppermute(head, axis, [((i + 1) % count, i) for i in range(ends)])  10.8 us
  transfers between devices with their start and end apart: 11, of which 5 were waited for; matrix products, arithmetic and copies ran while one was open for 6% of the time, Pallas kernels for 0%

commit v1 on v0

v1 whole, which is shorter than its diff:
```python
import jax
import jax.numpy as jnp
from jax import lax
from jax.experimental import pallas as pl
from jax.experimental.pallas import tpu as pltpu
from jax.sharding import PartitionSpec as P

MESH = pl.DeviceIdType.MESH
F32 = jnp.float32
BF16 = jnp.bfloat16


def extended(cells, sides, width):
    for axis, dim in sides:
        count = lax.axis_size(axis)
        ends = count - 1
        head = lax.slice_in_dim(cells, 0, width, axis=dim)
        tail = lax.slice_in_dim(cells, cells.shape[dim] - width, cells.shape[dim], axis=dim)
        cells = jnp.concatenate(
            [
                lax.ppermute(tail, axis, [(i, (i + 1) % count) for i in range(ends)]),
                cells,
                lax.ppermute(head, axis, [((i + 1) % count, i) for i in range(ends)]),
            ],
            axis=dim,
        )
    return cells


def tendency(padded, coefs, recv, gamma, keep):
    center = padded[:, 1:-1, 1:-1]
    xminus = padded[:, :-2, 1:-1]
    xplus = padded[:, 2:, 1:-1]
    yminus = padded[:, 1:-1, :-2]
    yplus = padded[:, 1:-1, 2:]
    speed_x = coefs[0]
    speed_y = coefs[1]
    kappa = coefs[2]
    advect = -(
        jnp.maximum(speed_x, 0.0) * (center - xminus) + jnp.minimum(speed_x, 0.0) * (xplus - center)
    )
    advect = advect - (
        jnp.maximum(speed_y, 0.0) * (center - yminus) + jnp.minimum(speed_y, 0.0) * (yplus - center)
    )
    diffuse = kappa * (xplus + xminus + yplus + yminus - 4.0 * center)
    chan = recv.shape[0]
    couple = gamma[:, None, None] * (recv - center[:chan])
    couple = jnp.concatenate([couple, jnp.zeros_like(center[chan:])], axis=0)
    return keep * (advect + diffuse + couple)


def shallow_rims(field):
    return extended(field, (("tx", 1), ("ty", 2)), 1)


TILES = 64
PAIRS = 512
CAP = 16
SLOTS = TILES * CAP
NB = 512
CH = 8


def plan_kernel(src, dev, blk, slot_k, slot_src, slot_id, count):
    def clear(i, carry):
        slot_k[i] = 0
        slot_src[i] = 0
        slot_id[i] = NB
        return carry

    lax.fori_loop(0, SLOTS, clear, 0, unroll=8)

    def clear_count(i, carry):
        count[i] = 0
        return carry

    lax.fori_loop(0, TILES, clear_count, 0, unroll=8)

    def place(k, carry):
        d = dev[k]
        r = count[d]
        count[d] = r + 1
        s = d * CAP + r
        b = blk[k]
        x = b >> 2
        slot_k[s] = k
        slot_src[s] = src[k]
        slot_id[s] = (x >> 3) * 32 + (b & 3) * 8 + (x & 7)
        return carry

    lax.fori_loop(0, PAIRS, place, 0, unroll=8)


def plan(src, dev, blk):
    smem = pl.BlockSpec(memory_space=pltpu.SMEM)
    return pl.pallas_call(
        plan_kernel,
        out_shape=[jax.ShapeDtypeStruct((SLOTS,), jnp.int32)] * 3,
        in_specs=[smem] * 3,
        out_specs=[smem] * 3,
        scratch_shapes=[pltpu.SMEM((TILES,), jnp.int32)],
    )(src, dev, blk)


def remap_kernel(
    slot_k,
    slot_src,
    ids,
    state,
    weights,
    out,
    wbuf,
    surf,
    send,
    recv,
    recv_ids,
    acc,
    wsem,
    ssem,
    rsem,
    isend,
    irecv,
):
    comp = lax.axis_index("comp")
    tx = lax.axis_index("tx")
    ty = lax.axis_index("ty")
    h = tx // 4
    x = tx % 4
    y = ty // 2
    core = ty % 2
    sign = 1 - 2 * core

    load = pltpu.make_async_copy(weights.at[0], wbuf, wsem)
    load.start()

    def partner(i):
        dh = lax.rem(i, 2)
        dx = lax.rem(lax.div(i, 2), 4)
        dy = lax.rem(lax.div(i, 8) + dx, 4)
        dc = lax.div(i, 32)
        to_x = lax.rem(h + dh, 2) * 4 + lax.rem(x + sign * dx + 4, 4)
        to_y = lax.rem(y + sign * dy + 4, 4) * 2 + lax.rem(core + dc, 2)
        return to_x, to_y

    barrier = pltpu.get_barrier_semaphore()

    def greet(i, carry):
        to_x, to_y = partner(i)
        pl.semaphore_signal(barrier, 1, device_id=(1 - comp, to_x, to_y), device_id_type=MESH)
        return carry

    lax.fori_loop(0, TILES, greet, 0)

    def relay(i, carry):
        for yb in range(4):
            rows = pl.ds(pl.multiple_of(i * 8, 8), 8)
            tiles = state[0, :, rows, yb * 128 : yb * 128 + 128]
            tiles = jnp.swapaxes(tiles, 0, 1)
            for r in range(8):
                surf[i * 32 + r * 4 + yb] = tiles[r]
        return carry

    lax.fori_loop(0, 16, relay, 0)
    pl.semaphore_wait(barrier, TILES)

    def copies(i):
        to_x, to_y = partner(i)
        to = (1 - comp, to_x, to_y)
        data = pltpu.make_async_remote_copy(
            send.at[i], recv.at[i], ssem.at[i], rsem.at[i], device_id=to, device_id_type=MESH
        )
        names = pltpu.make_async_remote_copy(
            ids.at[to_x * 8 + to_y],
            recv_ids.at[i],
            isend.at[i],
            irecv.at[i],
            device_id=to,
            device_id_type=MESH,
        )
        return data, names, to_x * 8 + to_y

    load.wait()

    def produce(i, carry):
        data, names, tile = copies(i)
        names.start()
        zero = jnp.zeros((8, 128), F32)
        for g in range(CAP // 4):
            ws = []
            ps = []
            for j in range(4):
                s = tile * CAP + g * 4 + j
                ws.append(wbuf[slot_k[s]])
                ps.append(surf[slot_src[s]])
            lhs = jnp.concatenate(
                [
                    jnp.concatenate([ps[0], zero, ps[2], zero], axis=0),
                    jnp.concatenate([zero, ps[1], zero, ps[3]], axis=0),
                ],
                axis=1,
            ).astype(BF16)
            rhs = jnp.concatenate(
                [
                    jnp.concatenate([ws[0], ws[1]], axis=1),
                    jnp.concatenate([ws[2], ws[3]], axis=1),
                ],
                axis=0,
            )
            both = lax.dot_general(
                lhs, rhs, (((1,), (1,)), ((), ())), preferred_element_type=F32
            )
            parts = [both[0:8, :128], both[8:16, :128], both[16:24, 128:], both[24:32, 128:]]
            for j in range(4):
                send[i, pl.ds(g * 4 + j, 8, stride=CAP), :] = parts[j]
        data.start()
        return carry

    lax.fori_loop(0, TILES, produce, 0)

    def arrive(i, carry):
        data, names, _ = copies(i)
        names.wait_recv()
        data.wait_recv()
        return carry

    seg = lax.broadcasted_iota(jnp.int32, (8, 128), 1) // CAP == lax.broadcasted_iota(
        jnp.int32, (8, 128), 0
    )
    for q in range(4):
        lax.fori_loop(16 * q, 16 * q + 16, arrive, 0)
        lanes = []
        for half in range(2):
            first = q * 16 + half * 8
            rows = jnp.concatenate([recv_ids[first + j] for j in range(8)], axis=0)
            lanes.append(jnp.sum(jnp.where(seg, rows, 0.0), axis=0, keepdims=True))
        wanted = jnp.concatenate(lanes, axis=1)
        blocks = lax.broadcasted_iota(jnp.int32, (NB, 256), 0).astype(F32)
        select = jnp.where(blocks == wanted, 1.0, 0.0).astype(BF16)
        for c in range(0, CH, 2):
            cols = []
            for cc in (c, c + 1):
                cols.append(
                    jnp.concatenate(
                        [recv[q * 16 + j, cc * CAP : cc * CAP + CAP, :] for j in range(16)], axis=0
                    )
                )
            terms = jnp.concatenate(cols, axis=1)
            high = terms.astype(BF16)
            low = (terms - high.astype(F32)).astype(BF16)
            total = jnp.dot(select, high, preferred_element_type=F32)
            total = total + jnp.dot(select, low, preferred_element_type=F32)
            for cc in range(2):
                piece = total[:, cc * 128 : cc * 128 + 128]
                if q == 0:
                    acc[c + cc] = piece
                else:
                    acc[c + cc] += piece

    def unfold(i, carry):
        for yb in range(4):
            for c in range(CH):
                out[c, pl.ds(pl.multiple_of(i * 8, 8), 8), yb * 128 : yb * 128 + 128] = acc[
                    c, pl.ds(pl.multiple_of(i * 32 + yb * 8, 8), 8), :
                ]
        return carry

    lax.fori_loop(0, 16, unfold, 0)

    def sent(i, carry):
        data, names, _ = copies(i)
        names.wait_send()
        data.wait_send()
        return carry

    lax.fori_loop(0, TILES, sent, 0)


def remap(slot_k, slot_src, ids, state, weights):
    smem = pl.BlockSpec(memory_space=pltpu.SMEM)
    vmem = pl.BlockSpec(memory_space=pltpu.VMEM)
    return pl.pallas_call(
        remap_kernel,
        grid=(1,),
        out_shape=jax.ShapeDtypeStruct((CH, 128, 512), F32),
        in_specs=[
            smem,
            smem,
            vmem,
            pl.BlockSpec((1, CH, 128, 512), lambda g: (0, 0, 0, 0)),
            pl.BlockSpec(memory_space=pl.ANY),
        ],
        out_specs=vmem,
        scratch_shapes=[
            pltpu.VMEM((PAIRS, 128, 128), BF16),
            pltpu.VMEM((NB, CH, 128), F32),
            pltpu.VMEM((TILES, CH * CAP, 128), F32),
            pltpu.VMEM((TILES, CH * CAP, 128), F32),
            pltpu.VMEM((TILES, 1, 128), F32),
            pltpu.VMEM((CH, NB, 128), F32),
            pltpu.SemaphoreType.DMA,
            pltpu.SemaphoreType.DMA((TILES,)),
            pltpu.SemaphoreType.DMA((TILES,)),
            pltpu.SemaphoreType.DMA((TILES,)),
            pltpu.SemaphoreType.DMA((TILES,)),
        ],
        compiler_params=pltpu.CompilerParams(
            collective_id=0, has_side_effects=True, vmem_limit_bytes=56 << 20
        ),
    )(slot_k, slot_src, ids, state, weights)


def body(state, coefs, land_sea, gamma, pair_src, pair_dev, pair_blk, weights):
    comp_index = lax.axis_index("comp")
    cells_x, cells_y = state.shape[2], state.shape[3]
    slot_k, slot_src, slot_id = plan(
        pair_src.reshape(PAIRS), pair_dev.reshape(PAIRS), pair_blk.reshape(PAIRS)
    )
    ids = jnp.tile(slot_id.astype(F32).reshape(TILES, 1, CAP), (1, 1, 8))
    recv = remap(slot_k, slot_src, ids, state, weights)
    is_atmos = comp_index == 0
    keep = jnp.where(
        is_atmos, jnp.ones((cells_x, cells_y), jnp.float32), land_sea.astype(jnp.float32)
    )
    mix_a = jnp.where(is_atmos, 0.0, 0.5).astype(jnp.float32)
    mix_b = jnp.where(is_atmos, 1.0, 0.5).astype(jnp.float32)
    start = state[0]
    local_coefs = coefs[0]
    rates = gamma[0]
    first = tendency(shallow_rims(start), local_coefs, recv, rates, keep)
    section = start + first
    second = tendency(shallow_rims(section), local_coefs, recv, rates, keep)
    result = mix_a * start + (1.0 - mix_a) * section + mix_b * second
    return (result[None], recv[None])


def solution(mesh):
    placed = (
        P("comp", None, "tx", "ty"),
        P("comp", None, "tx", "ty"),
        P("tx", "ty"),
        P("comp", None),
        P("comp", ("tx", "ty")),
        P("comp", ("tx", "ty"), None),
        P("comp", ("tx", "ty")),
        P("comp", ("tx", "ty"), None, None),
    )
    return jax.shard_map(
        body,
        mesh=mesh,
        in_specs=placed,
        out_specs=(P("comp", None, "tx", "ty"), P("comp", None, "tx", "ty")),
        check_vma=False,
    )
```

time: 338 us -> 178 us (0.53)
  the two profiles are of different devices: /device:TPU:9 before, /device:TPU:39 now
where the time goes in v1:
time: 178 us; the launch traced here: 177 us
  Pallas kernels  76.6 us (43%)
  other arithmetic  44.8 us (25%)
  starting transfers between devices  29.9 us (17%)
  local copies, waits for them, and re-layouts  18 us (10%)
  waiting for transfers between devices  6.65 us (4%)
    pallas_call x1, Pallas kernels, remap(): pl.pallas_call(remap_kernel, grid=(1,), out_shape=jax.ShapeDtypeStruct((C...  69 us
    ppermute x4, starting transfers between devices, extended(): lax.ppermute(tail, axis, [(i, (i + 1) % count) for i in range(ends)])  20.7 us
    broadcast_in_dim x1, other arithmetic, body(): return (result[None], recv[None])  15.8 us
    add x1, other arithmetic, body(): section = start + first  14.4 us
    ppermute x4, starting transfers between devices, extended(): lax.ppermute(head, axis, [((i + 1) % count, i) for i in range(ends)])  9.21 us
    pallas_call x1, Pallas kernels, plan(): pl.pallas_call(plan_kernel, out_shape=[jax.ShapeDtypeStruct((SLOTS,), jnp...  7.56 us
    ppermute x4, waiting for transfers between devices, extended(): lax.ppermute(head, axis, [((i + 1) % count, i) for i in range(ends)])  6.32 us
    slice x4, local copies, waits for them, and re-layouts, extended(): lax.slice_in_dim(cells, cells.shape[dim] - width, cells.shape[dim], axis=...  6.05 us
  transfers between devices with their start and end apart: 8, of which 2 were waited for; matrix products, arithmetic and copies ran while one was open for 7% of the time, Pallas kernels for 43%

profile of v1, /device:TPU:39, one launch (start us, length us, event | category | flops | bytes accessed | tf_op | source)
XLA Modules:
  0.0 176.7 jit_solution(8851014990982865572)
XLA Ops:
  0.6 1.1 fusion.37
  1.7 4.5 %collective-permute-start = (f32[16,1,512]{2,1,0:T(1,128)S(1)}, f32[16,1,512]{2,1,0:T(1,128)S(1)}, u32[]{:S(2)}, u32[]{:S(2)}) collective-permute-start(f32[16,1,512]{2,1,0:T(1,128)S(1)} %get-tuple-element.14), channel_id=1, source_target_pairs={{0,8},{8,16},{16,24},{24,32},{32,40},{40,48},{48,56},{1,9},{9,17},... | collective-permute-start | bytes 98312 | tf_op jit(solution)/shard_map/ppermute | solution.py:21
  6.2 1.9 %collective-permute-start.1 = (f32[16,1,512]{2,1,0:T(1,128)S(1)}, f32[16,1,512]{2,1,0:T(1,128)S(1)}, u32[]{:S(2)}, u32[]{:S(2)}) collective-permute-start(f32[16,1,512]{2,1,0:T(1,128)S(1)} %get-tuple-element.15), channel_id=1, source_target_pairs={{8,0},{16,8},{24,16},{32,24},{40,32},{48,40},{56,48},{9,1},{17,9},... | collective-permute-start | bytes 98312 | tf_op jit(solution)/shard_map/ppermute | solution.py:23
  8.2 7.6 %shard_map.95 = (s32[1024]{0:T(1024)}, s32[1024]{0:T(1024)}, s32[1024]{0:T(1024)}) custom-call(s32[512]{0:T(512)} %bitcast.31, s32[512]{0:T(512)} %bitcast.32, s32[512]{0:T(512)} %bitcast.33), custom_call_target="tpu_custom_call" | custom-call | tf_op jit(solution)/shard_map/pallas_call | solution.py:96
  15.7 0.7 convert_element_type.7
  16.4 0.1 tile.10
  16.5 0.1 copy.16
  16.6 0.7 copy.17.ids
  17.3 0.0 copy-start
  17.3 0.0 copy-start.4
  17.3 69.0 %shard_map.96 = f32[8,128,512]{2,1,0:T(8,128)} custom-call(s32[1024]{0:T(1024)} %get-tuple-element.5.slot_k, s32[1024]{0:T(1024)} %get-tuple-element.6.slot_src, f32[64,1,128]{2,1,0:T(1,128)} %copy.17.ids, f32[1,16,128,512]{3,2,1,0:T(8,128)} %state.1, bf16[1,512,128,128]{3,2,1,0:T(8,128)(2,1)} %weights.1), custom_call_target="tpu_custom_call" | custom-call | tf_op jit(solution)/shard_map/pallas_call | solution.py:281
  86.3 0.0 copy-start.3
  86.3 0.0 copy-done
  86.3 0.0 copy-done.4
  86.4 2.3 %fusion.35 = f32[8,128,512]{2,1,0:T(8,128)S(1)} fusion(f32[8,128,512]{2,1,0:T(8,128)} %shard_map.96, f32[1,16,128,512]{3,2,1,0:T(8,128)S(1)} %copy-done, f32[8]{0:T(128)S(1)} %bitcast.30), kind=kLoop, calls=%fused_computation.53 | loop fusion | flops 1048576 | bytes 6291488 | tf_op jit(solution)/shard_map/mul | solution.py:47
  88.7 0.0 copy-done.3
  88.7 1.1 maximum_bitcast_fusion.1
  89.8 0.0 collective-permute-done
  89.8 0.0 collective-permute-done.1
  89.8 3.0 %pad_maximum_fusion.21 = (f32[16,130,1]{2,1,0:T(8,128)}, f32[16,130,1]{2,1,0:T(8,128)S(1)}) fusion(f32[16,1,512]{2,1,0:T(1,128)S(1)} %collective-permute-done.1, f32[16,128,512]{2,1,0:T(8,128)} %bitcast.25, f32[16,1,512]{2,1,0:T(1,128)S(1)} %collective-permute-done), kind=kLoop, calls=%fused_computation.59 | loop fusion | flops 8320 | bytes 4276480 | tf_op jit(solution)/shard_map/slice | solution.py:18
  92.8 2.5 %copy.12 = f32[16,130,1]{1,0,2:T(8,128)} copy(f32[16,130,1]{2,1,0:T(8,128)} %get-tuple-element.10) | data formatting | bytes 16640 | tf_op jit(solution)/shard_map/slice | solution.py:18
  95.3 0.6 copy.14
  95.9 3.4 %collective-permute-start.3 = (f32[16,130,1]{1,0,2:T(8,128)S(1)}, f32[16,130,1]{1,0,2:T(8,128)}, u32[]{:S(2)}, u32[]{:S(2)}) collective-permute-start(f32[16,130,1]{1,0,2:T(8,128)S(1)} %copy.14), channel_id=1, source_target_pairs={{1,0},{2,1},{3,2},{4,3},{5,4},{6,5},{7,6},{9,8},{10,9},{11,10},{12... | collective-permute-start | bytes 24968 | tf_op jit(solution)/shard_map/ppermute | solution.py:23
  99.3 2.1 %collective-permute-start.2 = (f32[16,130,1]{1,0,2:T(8,128)}, f32[16,130,1]{1,0,2:T(8,128)}, u32[]{:S(2)}, u32[]{:S(2)}) collective-permute-start(f32[16,130,1]{1,0,2:T(8,128)} %copy.12), channel_id=1, source_target_pairs={{0,1},{1,2},{2,3},{3,4},{4,5},{5,6},{6,7},{8,9},{9,10},{10,11},{11... | collective-permute-start | bytes 24968 | tf_op jit(solution)/shard_map/ppermute | solution.py:21
  101.4 1.0 convert_select_fusion
  102.4 0.3 collective-permute-done.2
  102.7 1.1 copy.13
  103.9 0.0 collective-permute-done.3
  103.9 2.1 %copy.15 = f32[16,130,1]{2,1,0:T(8,128)} copy(f32[16,130,1]{1,0,2:T(8,128)} %collective-permute-done.3) | data formatting | bytes 16640 | tf_op jit(solution)/shard_map/ppermute | solution.py:23
  106.0 14.4 %fusion.27 = f32[16,128,512]{2,1,0:T(8,128)S(1)} fusion(f32[16,128,512]{2,1,0:T(8,128)} %bitcast.26, f32[16,1,512]{2,1,0:T(1,128)S(1)} %collective-permute-done.1, f32[16,1,512]{2,1,0:T(1,128)S(1)} %collective-permute-done, f32[8,128,512]{2,1,0:T(8,128)S(1)} %fusion.35, f32[16,130,1]{2,1,0:T(8,128)} %copy.15, f32[16,130,1]{2,1,0:T(8,128)S(1)} %copy.13, ...), kind=kLoop, calls=%fused_computation.42 | loop fusion | flops 31457280 | bytes 12140800 | tf_op jit(solution)/shard_map/add | solution.py:330
  120.5 0.0 copy-start.1
  120.5 1.9 %copy-done.1 = f32[16,128,512]{2,1,0:T(8,128)} copy-done((f32[16,128,512]{2,1,0:T(8,128)}, f32[16,128,512]{2,1,0:T(8,128)S(1)}, u32[]{:S(2)}) %copy-start.1) | copy-done | bytes 4194328
  122.4 0.1 fusion.36
  122.5 8.2 %collective-permute-start.4 = (f32[16,1,512]{2,1,0:T(1,128)S(1)}, f32[16,1,512]{2,1,0:T(1,128)S(1)}, u32[]{:S(2)}, u32[]{:S(2)}) collective-permute-start(f32[16,1,512]{2,1,0:T(1,128)S(1)} %get-tuple-element.12), channel_id=1, source_target_pairs={{0,8},{8,16},{16,24},{24,32},{32,40},{40,48},{48,56},{1,9},{9,17},... | collective-permute-start | bytes 98312 | tf_op jit(solution)/shard_map/ppermute | solution.py:21
  130.6 1.9 %collective-permute-start.5 = (f32[16,1,512]{2,1,0:T(1,128)S(1)}, f32[16,1,512]{2,1,0:T(1,128)S(1)}, u32[]{:S(2)}, u32[]{:S(2)}) collective-permute-start(f32[16,1,512]{2,1,0:T(1,128)S(1)} %get-tuple-element.13), channel_id=1, source_target_pairs={{8,0},{16,8},{24,16},{32,24},{40,32},{48,40},{56,48},{9,1},{17,9},... | collective-permute-start | bytes 98312 | tf_op jit(solution)/shard_map/ppermute | solution.py:23
  132.6 0.0 copy-start.2
  132.6 0.0 collective-permute-done.4
  132.6 6.3 %collective-permute-done.5 = f32[16,1,512]{2,1,0:T(1,128)S(1)} collective-permute-done((f32[16,1,512]{2,1,0:T(1,128)S(1)}, f32[16,1,512]{2,1,0:T(1,128)S(1)}, u32[]{:S(2)}, u32[]{:S(2)}) %collective-permute-start.5) | collective-permute-done | bytes 32800 | tf_op jit(solution)/shard_map/ppermute | solution.py:23
  138.9 3.0 %pad_maximum_fusion.18 = (f32[16,130,1]{2,1,0:T(8,128)}, f32[16,130,1]{2,1,0:T(8,128)S(1)}) fusion(f32[16,1,512]{2,1,0:T(1,128)S(1)} %collective-permute-done.5, f32[16,128,512]{2,1,0:T(8,128)} %copy-done.1, f32[16,1,512]{2,1,0:T(1,128)S(1)} %collective-permute-done.4), kind=kLoop, calls=%fused_computation.56 | loop fusion | flops 8320 | bytes 4276480 | tf_op jit(solution)/shard_map/slice | solution.py:18
  141.9 2.5 %copy.18 = f32[16,130,1]{1,0,2:T(8,128)} copy(f32[16,130,1]{2,1,0:T(8,128)} %get-tuple-element.8) | data formatting | bytes 16640 | tf_op jit(solution)/shard_map/slice | solution.py:18
  144.3 0.6 copy.20
  144.9 1.9 %collective-permute-start.7 = (f32[16,130,1]{1,0,2:T(8,128)S(1)}, f32[16,130,1]{1,0,2:T(8,128)}, u32[]{:S(2)}, u32[]{:S(2)}) collective-permute-start(f32[16,130,1]{1,0,2:T(8,128)S(1)} %copy.20), channel_id=1, source_target_pairs={{1,0},{2,1},{3,2},{4,3},{5,4},{6,5},{7,6},{9,8},{10,9},{11,10},{12... | collective-permute-start | bytes 24968 | tf_op jit(solution)/shard_map/ppermute | solution.py:23
  146.9 5.9 %collective-permute-start.6 = (f32[16,130,1]{1,0,2:T(8,128)}, f32[16,130,1]{1,0,2:T(8,128)}, u32[]{:S(2)}, u32[]{:S(2)}) collective-permute-start(f32[16,130,1]{1,0,2:T(8,128)} %copy.18), channel_id=1, source_target_pairs={{0,1},{1,2},{2,3},{3,4},{4,5},{5,6},{6,7},{8,9},{9,10},{10,11},{11... | collective-permute-start | bytes 24968 | tf_op jit(solution)/shard_map/ppermute | solution.py:21
  152.8 0.0 copy-done.2
  152.8 3.5 %fusion.34 = f32[8,128,512]{2,1,0:T(8,128)} fusion(f32[8,128,512]{2,1,0:T(8,128)S(1)} %copy-done.2, f32[16,128,512]{2,1,0:T(8,128)} %copy-done.1, f32[8]{0:T(128)} %bitcast.29), kind=kLoop, calls=%fused_computation.51 | loop fusion | flops 1048576 | bytes 6291488 | tf_op jit(solution)/shard_map/mul | solution.py:47
  156.3 0.0 collective-permute-done.6
  156.3 1.1 copy.19
  157.5 0.0 collective-permute-done.7
  157.5 2.2 %copy.21 = f32[16,130,1]{2,1,0:T(8,128)} copy(f32[16,130,1]{1,0,2:T(8,128)} %collective-permute-done.7) | data formatting | bytes 16640 | tf_op jit(solution)/shard_map/ppermute | solution.py:23
  159.6 15.8 %fusion.11 = f32[1,16,128,512]{3,2,1,0:T(8,128)} fusion(f32[16,1,512]{2,1,0:T(1,128)S(1)} %collective-permute-done.5, f32[16,128,512]{2,1,0:T(8,128)} %copy-done.1, f32[16,1,512]{2,1,0:T(1,128)S(1)} %collective-permute-done.4, f32[8,128,512]{2,1,0:T(8,128)} %fusion.34, f32[16,130,1]{2,1,0:T(8,128)} %copy.21, f32[16,130,1]{2,1,0:T(8,128)S(1)} %copy.19, ...), kind=kLoop, calls=%fused_computation.18 | loop fusion | flops 35651584 | bytes 16335116 | tf_op jit(solution)/shard_map/broadcast_in_dim | solution.py:333
  175.4 1.3 copy.23
  (1 shorter events, 0.0 us)
Async XLA Ops:
  1.7 88.1 %collective-permute-start = (f32[16,1,512]{2,1,0:T(1,128)S(1)}, f32[16,1,512]{2,1,0:T(1,128)S(1)}, u32[]{:S(2)}, u32[]{:S(2)}) collective-permute-start(f32[16,1,512]{2,1,0:T(1,128)S(1)} %get-tuple-element.14), channel_id=1, source_target_pairs={{0,8},{8,16},{16,24},{24,32},{32,40},{40,48},{48,56},{1,9},{9,17},... | collective-permute-start | bytes 98312 | tf_op jit(solution)/shard_map/ppermute | solution.py:21
  6.2 83.6 %collective-permute-start.1 = (f32[16,1,512]{2,1,0:T(1,128)S(1)}, f32[16,1,512]{2,1,0:T(1,128)S(1)}, u32[]{:S(2)}, u32[]{:S(2)}) collective-permute-start(f32[16,1,512]{2,1,0:T(1,128)S(1)} %get-tuple-element.15), channel_id=1, source_target_pairs={{8,0},{16,8},{24,16},{32,24},{40,32},{48,40},{56,48},{9,1},{17,9},... | collective-permute-start | bytes 98312 | tf_op jit(solution)/shard_map/ppermute | solution.py:23
  17.3 69.0 %copy-start = (f32[1,16,128,512]{3,2,1,0:T(8,128)S(1)}, f32[1,16,128,512]{3,2,1,0:T(8,128)}, u32[]{:S(2)}) copy-start(f32[1,16,128,512]{3,2,1,0:T(8,128)} %state.1) | copy-start | bytes 12582916
  17.3 69.0 %copy-start.4 = (f32[1,8]{1,0:T(1,128)S(1)}, f32[1,8]{1,0:T(1,128)}, u32[]{:S(2)}) copy-start(f32[1,8]{1,0:T(1,128)} %param.11) | copy-start | bytes 100
  86.3 2.4 %copy-start.3 = (f32[1,3,128,512]{3,2,1,0:T(8,128)S(1)}, f32[1,3,128,512]{3,2,1,0:T(8,128)}, u32[]{:S(2)}) copy-start(f32[1,3,128,512]{3,2,1,0:T(8,128)} %param.9) | copy-start | bytes 2359300
  95.9 8.0 %collective-permute-start.3 = (f32[16,130,1]{1,0,2:T(8,128)S(1)}, f32[16,130,1]{1,0,2:T(8,128)}, u32[]{:S(2)}, u32[]{:S(2)}) collective-permute-start(f32[16,130,1]{1,0,2:T(8,128)S(1)} %copy.14), channel_id=1, source_target_pairs={{1,0},{2,1},{3,2},{4,3},{5,4},{6,5},{7,6},{9,8},{10,9},{11,10},{12... | collective-permute-start | bytes 24968 | tf_op jit(solution)/shard_map/ppermute | solution.py:23
  99.3 3.4 %collective-permute-start.2 = (f32[16,130,1]{1,0,2:T(8,128)}, f32[16,130,1]{1,0,2:T(8,128)}, u32[]{:S(2)}, u32[]{:S(2)}) collective-permute-start(f32[16,130,1]{1,0,2:T(8,128)} %copy.12), channel_id=1, source_target_pairs={{0,1},{1,2},{2,3},{3,4},{4,5},{5,6},{6,7},{8,9},{9,10},{10,11},{11... | collective-permute-start | bytes 24968 | tf_op jit(solution)/shard_map/ppermute | solution.py:21
  120.5 2.0 %copy-start.1 = (f32[16,128,512]{2,1,0:T(8,128)}, f32[16,128,512]{2,1,0:T(8,128)S(1)}, u32[]{:S(2)}) copy-start(f32[16,128,512]{2,1,0:T(8,128)S(1)} %fusion.27) | copy-start | bytes 12582916
  122.5 10.1 %collective-permute-start.4 = (f32[16,1,512]{2,1,0:T(1,128)S(1)}, f32[16,1,512]{2,1,0:T(1,128)S(1)}, u32[]{:S(2)}, u32[]{:S(2)}) collective-permute-start(f32[16,1,512]{2,1,0:T(1,128)S(1)} %get-tuple-element.12), channel_id=1, source_target_pairs={{0,8},{8,16},{16,24},{24,32},{32,40},{40,48},{48,56},{1,9},{9,17},... | collective-permute-start | bytes 98312 | tf_op jit(solution)/shard_map/ppermute | solution.py:21
  130.6 8.3 %collective-permute-start.5 = (f32[16,1,512]{2,1,0:T(1,128)S(1)}, f32[16,1,512]{2,1,0:T(1,128)S(1)}, u32[]{:S(2)}, u32[]{:S(2)}) collective-permute-start(f32[16,1,512]{2,1,0:T(1,128)S(1)} %get-tuple-element.13), channel_id=1, source_target_pairs={{8,0},{16,8},{24,16},{32,24},{40,32},{48,40},{56,48},{9,1},{17,9},... | collective-permute-start | bytes 98312 | tf_op jit(solution)/shard_map/ppermute | solution.py:23
  132.6 20.2 %copy-start.2 = (f32[8,128,512]{2,1,0:T(8,128)S(1)}, f32[8,128,512]{2,1,0:T(8,128)}, u32[]{:S(2)}) copy-start(f32[8,128,512]{2,1,0:T(8,128)} %shard_map.96) | copy-start | bytes 6291460
  144.9 12.5 %collective-permute-start.7 = (f32[16,130,1]{1,0,2:T(8,128)S(1)}, f32[16,130,1]{1,0,2:T(8,128)}, u32[]{:S(2)}, u32[]{:S(2)}) collective-permute-start(f32[16,130,1]{1,0,2:T(8,128)S(1)} %copy.20), channel_id=1, source_target_pairs={{1,0},{2,1},{3,2},{4,3},{5,4},{6,5},{7,6},{9,8},{10,9},{11,10},{12... | collective-permute-start | bytes 24968 | tf_op jit(solution)/shard_map/ppermute | solution.py:23
  146.9 9.4 %collective-permute-start.6 = (f32[16,130,1]{1,0,2:T(8,128)}, f32[16,130,1]{1,0,2:T(8,128)}, u32[]{:S(2)}, u32[]{:S(2)}) collective-permute-start(f32[16,130,1]{1,0,2:T(8,128)} %copy.18), channel_id=1, source_target_pairs={{0,1},{1,2},{2,3},{3,4},{4,5},{5,6},{6,7},{8,9},{9,10},{10,11},{11... | collective-permute-start | bytes 24968 | tf_op jit(solution)/shard_map/ppermute | solution.py:21

commit v2 on v1

--- a/solution.py
+++ b/solution.py
@@ -10,55 +10,15 @@
 BF16 = jnp.bfloat16
 
 
-def extended(cells, sides, width):
-    for axis, dim in sides:
-        count = lax.axis_size(axis)
-        ends = count - 1
-        head = lax.slice_in_dim(cells, 0, width, axis=dim)
-        tail = lax.slice_in_dim(cells, cells.shape[dim] - width, cells.shape[dim], axis=dim)
-        cells = jnp.concatenate(
-            [
-                lax.ppermute(tail, axis, [(i, (i + 1) % count) for i in range(ends)]),
-                cells,
-                lax.ppermute(head, axis, [((i + 1) % count, i) for i in range(ends)]),
-            ],
-            axis=dim,
-        )
-    return cells
-
-
-def tendency(padded, coefs, recv, gamma, keep):
-    center = padded[:, 1:-1, 1:-1]
-    xminus = padded[:, :-2, 1:-1]
-    xplus = padded[:, 2:, 1:-1]
-    yminus = padded[:, 1:-1, :-2]
-    yplus = padded[:, 1:-1, 2:]
-    speed_x = coefs[0]
-    speed_y = coefs[1]
-    kappa = coefs[2]
-    advect = -(
-        jnp.maximum(speed_x, 0.0) * (center - xminus) + jnp.minimum(speed_x, 0.0) * (xplus - center)
-    )
-    advect = advect - (
-        jnp.maximum(speed_y, 0.0) * (center - yminus) + jnp.minimum(speed_y, 0.0) * (yplus - center)
-    )
-    diffuse = kappa * (xplus + xminus + yplus + yminus - 4.0 * center)
-    chan = recv.shape[0]
-    couple = gamma[:, None, None] * (recv - center[:chan])
-    couple = jnp.concatenate([couple, jnp.zeros_like(center[chan:])], axis=0)
-    return keep * (advect + diffuse + couple)
-
-
-def shallow_rims(field):
-    return extended(field, (("tx", 1), ("ty", 2)), 1)
-
-
 TILES = 64
 PAIRS = 512
 CAP = 16
 SLOTS = TILES * CAP
 NB = 512
 CH = 8
+NF = 16
+CX = 128
+CY = 512
 
 
 def plan_kernel(src, dev, blk, slot_k, slot_src, slot_id, count):
@@ -102,24 +62,73 @@
     )(src, dev, blk)
 
 
+def slopes(i, coefs, land, comp, kc):
+    rows = pl.ds(pl.multiple_of(i * 8, 8), 8)
+    u = coefs[0, 0, rows, :]
+    v = coefs[0, 1, rows, :]
+    kappa = coefs[0, 2, rows, :]
+    keep = jnp.where(comp == 0, 1.0, land[rows, :].astype(F32))
+    kc[0, rows, :] = keep * (jnp.maximum(u, 0.0) + kappa)
+    kc[1, rows, :] = keep * (kappa - jnp.minimum(u, 0.0))
+    kc[2, rows, :] = keep * (jnp.maximum(v, 0.0) + kappa)
+    kc[3, rows, :] = keep * (kappa - jnp.minimum(v, 0.0))
+    kc[4, rows, :] = -keep * (jnp.abs(u) + jnp.abs(v) + 4.0 * kappa)
+    kc[5, rows, :] = keep
+
+
+def stencil(cur, prev, nxt, left, right, weight):
+    sub = lax.broadcasted_iota(jnp.int32, (8, CY), 0)
+    lane = lax.broadcasted_iota(jnp.int32, (8, CY), 1)
+    up = jnp.where(sub == 0, pltpu.roll(prev, 1, 0), pltpu.roll(cur, 1, 0))
+    down = jnp.where(sub == 7, pltpu.roll(nxt, 7, 0), pltpu.roll(cur, 7, 0))
+    back = jnp.where(lane == 0, left, pltpu.roll(cur, 1, 1))
+    ahead = jnp.where(lane == CY - 1, right, pltpu.roll(cur, CY - 1, 1))
+    total = weight[0] * up + weight[1] * down
+    total = total + (weight[2] * back + weight[3] * ahead)
+    return total + weight[4] * cur
+
+
+def mixes(comp):
+    a = jnp.where(comp == 0, 0.0, 0.5).astype(F32)
+    b = jnp.where(comp == 0, 1.0, 0.5).astype(F32)
+    return a, b
+
+
 def remap_kernel(
     slot_k,
     slot_src,
+    gamma,
     ids,
+    coefs,
+    land,
     state,
     weights,
     out,
+    section,
+    rest,
+    halo_x,
+    halo_y,
     wbuf,
     surf,
     send,
     recv,
     recv_ids,
     acc,
-    wsem,
+    sp,
+    sq,
+    part,
+    kc,
+    xs,
+    xr,
+    ys,
+    yr,
+    lsem,
     ssem,
     rsem,
     isend,
     irecv,
+    esend,
+    erecv,
 ):
     comp = lax.axis_index("comp")
     tx = lax.axis_index("tx")
@@ -130,7 +139,9 @@
     core = ty % 2
     sign = 1 - 2 * core
 
-    load = pltpu.make_async_copy(weights.at[0], wbuf, wsem)
+    load_state = pltpu.make_async_copy(state.at[0], sp.at[:, 8 : 8 + CX, :], lsem.at[0])
+    load_state.start()
+    load = pltpu.make_async_copy(weights.at[0], wbuf, lsem.at[1])
     load.start()
 
     def partner(i):
@@ -142,6 +153,13 @@
         to_y = lax.rem(y + sign * dy + 4, 4) * 2 + lax.rem(core + dc, 2)
         return to_x, to_y
 
+    beside = (
+        (comp, lax.rem(tx + 1, 8), ty),
+        (comp, lax.rem(tx + 7, 8), ty),
+        (comp, tx, lax.rem(ty + 1, 8)),
+        (comp, tx, lax.rem(ty + 7, 8)),
+    )
+
     barrier = pltpu.get_barrier_semaphore()
 
     def greet(i, carry):
@@ -150,18 +168,81 @@
         return carry
 
     lax.fori_loop(0, TILES, greet, 0)
+    for to in beside:
+        pl.semaphore_signal(barrier, 1, device_id=to, device_id_type=MESH)
+
+    def prepare(i, carry):
+        slopes(i, coefs, land, comp, kc)
+        return carry
+
+    lax.fori_loop(0, 16, prepare, 0)
+    load_state.wait()
 
     def relay(i, carry):
         for yb in range(4):
-            rows = pl.ds(pl.multiple_of(i * 8, 8), 8)
-            tiles = state[0, :, rows, yb * 128 : yb * 128 + 128]
+            rows = pl.ds(pl.multiple_of(i * 8 + 8, 8), 8)
+            tiles = sp[0:CH, rows, yb * 128 : yb * 128 + 128]
             tiles = jnp.swapaxes(tiles, 0, 1)
             for r in range(8):
                 surf[i * 32 + r * 4 + yb] = tiles[r]
         return carry
 
     lax.fori_loop(0, 16, relay, 0)
-    pl.semaphore_wait(barrier, TILES)
+
+    def edges(e):
+        moves = []
+        for n in range(4):
+            count = NF if e == 0 else CH
+            if n < 2:
+                box = (xs.at[e, n, 0:count], xr.at[e, n, 0:count])
+            else:
+                box = (ys.at[e, n - 2], yr.at[e, n - 2])
+            moves.append(
+                pltpu.make_async_remote_copy(
+                    box[0],
+                    box[1],
+                    esend.at[e, n],
+                    erecv.at[e, n],
+                    device_id=beside[n],
+                    device_id_type=MESH,
+                )
+            )
+        return moves
+
+    lanes = lax.broadcasted_iota(jnp.int32, (8, 128), 1)
+
+    def pack_columns(e, i, strips):
+        first = jnp.zeros((8, 128), F32)
+        last = jnp.zeros((8, 128), F32)
+        for f, cells in enumerate(strips):
+            first = jnp.where(lanes == f, cells[:, 0:1], first)
+            last = jnp.where(lanes == f, cells[:, -1:], last)
+        rows = pl.ds(pl.multiple_of(i * 8, 8), 8)
+        ys[e, 0, rows, :] = last
+        ys[e, 1, rows, :] = first
+
+    def settle(e):
+        for move in edges(e):
+            move.wait_recv()
+        for n, (place, end) in enumerate(((tx, 0), (tx, 7))):
+            count = NF if e == 0 else CH
+            xr[e, n, 0:count] = jnp.where(place == end, 0.0, xr[e, n, 0:count])
+        for n, (place, end) in enumerate(((ty, 0), (ty, 7))):
+            yr[e, n] = jnp.where(place == end, 0.0, yr[e, n])
+
+    def pack_state(i, carry):
+        rows = pl.ds(pl.multiple_of(i * 8 + 8, 8), 8)
+        pack_columns(0, i, [sp[f, rows, :] for f in range(NF)])
+        return carry
+
+    lax.fori_loop(0, 16, pack_state, 0)
+    for f in range(NF):
+        xs[0, 0, f : f + 1, :] = sp[f, 7 + CX : 8 + CX, :]
+        xs[0, 1, f : f + 1, :] = sp[f, 8:9, :]
+
+    pl.semaphore_wait(barrier, TILES + 4)
+    for move in edges(0):
+        move.start()
 
     def copies(i):
         to_x, to_y = partner(i)
@@ -217,6 +298,57 @@
 
     lax.fori_loop(0, TILES, produce, 0)
 
+    mix_a, mix_b = mixes(comp)
+    settle(0)
+    for f in range(NF):
+        sp[f, 7:8, :] = xr[0, 0, f : f + 1, :]
+        sp[f, 8 + CX : 9 + CX, :] = xr[0, 1, f : f + 1, :]
+
+    def around(box, f, i):
+        return [box[f, pl.ds(pl.multiple_of(i * 8 + o, 8), 8), :] for o in (8, 0, 16)]
+
+    def first_step(i, carry):
+        rows = pl.ds(pl.multiple_of(i * 8, 8), 8)
+        weight = [kc[n, rows, :] for n in range(5)]
+        keep = kc[5, rows, :]
+        left, right = yr[0, 0, rows, :], yr[0, 1, rows, :]
+        strips = []
+        for f in range(NF):
+            cur, prev, nxt = around(sp, f, i)
+            rate = stencil(cur, prev, nxt, left[:, f : f + 1], right[:, f : f + 1], weight)
+            if f < CH:
+                part[f, rows, :] = cur + (rate - (gamma[0, f] * keep) * cur)
+            else:
+                moved = cur + rate
+                sq[f - CH, pl.ds(pl.multiple_of(i * 8 + 8, 8), 8), :] = moved
+                strips.append(moved)
+        pack_columns(1, i, strips)
+        return carry
+
+    lax.fori_loop(0, 16, first_step, 0)
+    for f in range(CH):
+        xs[1, 0, f : f + 1, :] = sq[f, 7 + CX : 8 + CX, :]
+        xs[1, 1, f : f + 1, :] = sq[f, 8:9, :]
+    for move in edges(1):
+        move.start()
+    settle(1)
+    for f in range(CH):
+        sq[f, 7:8, :] = xr[1, 0, f : f + 1, :]
+        sq[f, 8 + CX : 9 + CX, :] = xr[1, 1, f : f + 1, :]
+
+    def second_step(i, carry):
+        rows = pl.ds(pl.multiple_of(i * 8, 8), 8)
+        weight = [kc[n, rows, :] for n in range(5)]
+        left, right = yr[1, 0, rows, :], yr[1, 1, rows, :]
+        for f in range(CH):
+            cur, prev, nxt = around(sq, f, i)
+            rate = stencil(cur, prev, nxt, left[:, f : f + 1], right[:, f : f + 1], weight)
+            start = sp[f + CH, pl.ds(pl.multiple_of(i * 8 + 8, 8), 8), :]
+            rest[f, rows, :] = mix_a * start + (1.0 - mix_a) * cur + mix_b * rate
+        return carry
+
+    lax.fori_loop(0, 16, second_step, 0)
+
     def arrive(i, carry):
         data, names, _ = copies(i)
         names.wait_recv()
@@ -228,12 +360,12 @@
     )
     for q in range(4):
         lax.fori_loop(16 * q, 16 * q + 16, arrive, 0)
-        lanes = []
+        names = []
         for half in range(2):
             first = q * 16 + half * 8
             rows = jnp.concatenate([recv_ids[first + j] for j in range(8)], axis=0)
-            lanes.append(jnp.sum(jnp.where(seg, rows, 0.0), axis=0, keepdims=True))
-        wanted = jnp.concatenate(lanes, axis=1)
+            names.append(jnp.sum(jnp.where(seg, rows, 0.0), axis=0, keepdims=True))
+        wanted = jnp.concatenate(names, axis=1)
         blocks = lax.broadcasted_iota(jnp.int32, (NB, 256), 0).astype(F32)
         select = jnp.where(blocks == wanted, 1.0, 0.0).astype(BF16)
         for c in range(0, CH, 2):
@@ -256,15 +388,28 @@
                 else:
                     acc[c + cc] += piece
 
-    def unfold(i, carry):
-        for yb in range(4):
-            for c in range(CH):
-                out[c, pl.ds(pl.multiple_of(i * 8, 8), 8), yb * 128 : yb * 128 + 128] = acc[
-                    c, pl.ds(pl.multiple_of(i * 32 + yb * 8, 8), 8), :
-                ]
-        return carry
-
-    lax.fori_loop(0, 16, unfold, 0)
+    def couple(i, carry):
+        rows = pl.ds(pl.multiple_of(i * 8, 8), 8)
+        keep = kc[5, rows, :]
+        strips = []
+        for f in range(CH):
+            cells = jnp.concatenate(
+                [acc[f, pl.ds(pl.multiple_of(i * 32 + yb * 8, 8), 8), :] for yb in range(4)],
+                axis=1,
+            )
+            out[f, rows, :] = cells
+            moved = part[f, rows, :] + (gamma[0, f] * keep) * cells
+            section[f, rows, :] = moved
+            strips.append(moved)
+        pack_columns(2, i, strips)
+        return carry
+
+    lax.fori_loop(0, 16, couple, 0)
+    for f in range(CH):
+        xs[2, 0, f : f + 1, :] = section[f, CX - 1 : CX, :]
+        xs[2, 1, f : f + 1, :] = section[f, 0:1, :]
+    for move in edges(2):
+        move.start()
 
     def sent(i, carry):
         data, names, _ = copies(i)
@@ -273,23 +418,31 @@
         return carry
 
     lax.fori_loop(0, TILES, sent, 0)
-
-
-def remap(slot_k, slot_src, ids, state, weights):
+    settle(2)
+    for n in range(2):
+        halo_x[n] = xr[2, n, 0:CH, :]
+        halo_y[n] = yr[2, n]
+    for e in range(3):
+        for move in edges(e):
+            move.wait_send()
+
+
+def remap(slot_k, slot_src, gamma, ids, coefs, land, state, weights):
     smem = pl.BlockSpec(memory_space=pltpu.SMEM)
     vmem = pl.BlockSpec(memory_space=pltpu.VMEM)
+    hbm = pl.BlockSpec(memory_space=pl.ANY)
+    half = jax.ShapeDtypeStruct((CH, CX, CY), F32)
     return pl.pallas_call(
         remap_kernel,
-        grid=(1,),
-        out_shape=jax.ShapeDtypeStruct((CH, 128, 512), F32),
-        in_specs=[
-            smem,
-            smem,
-            vmem,
-            pl.BlockSpec((1, CH, 128, 512), lambda g: (0, 0, 0, 0)),
-            pl.BlockSpec(memory_space=pl.ANY),
+        out_shape=[
+            half,
+            half,
+            half,
+            jax.ShapeDtypeStruct((2, CH, CY), F32),
+            jax.ShapeDtypeStruct((2, CX, 128), F32),
         ],
-        out_specs=vmem,
+        in_specs=[smem, smem, smem, vmem, vmem, vmem, hbm, hbm],
+        out_specs=[vmem] * 5,
         scratch_shapes=[
             pltpu.VMEM((PAIRS, 128, 128), BF16),
             pltpu.VMEM((NB, CH, 128), F32),
@@ -297,40 +450,106 @@
             pltpu.VMEM((TILES, CH * CAP, 128), F32),
             pltpu.VMEM((TILES, 1, 128), F32),
             pltpu.VMEM((CH, NB, 128), F32),
-            pltpu.SemaphoreType.DMA,
+            pltpu.VMEM((NF, CX + 16, CY), F32),
+            pltpu.VMEM((CH, CX + 16, CY), F32),
+            pltpu.VMEM((CH, CX, CY), F32),
+            pltpu.VMEM((6, CX, CY), F32),
+            pltpu.VMEM((3, 2, NF, CY), F32),
+            pltpu.VMEM((3, 2, NF, CY), F32),
+            pltpu.VMEM((3, 2, CX, 128), F32),
+            pltpu.VMEM((3, 2, CX, 128), F32),
+            pltpu.SemaphoreType.DMA((2,)),
             pltpu.SemaphoreType.DMA((TILES,)),
             pltpu.SemaphoreType.DMA((TILES,)),
             pltpu.SemaphoreType.DMA((TILES,)),
             pltpu.SemaphoreType.DMA((TILES,)),
+            pltpu.SemaphoreType.DMA((3, 4)),
+            pltpu.SemaphoreType.DMA((3, 4)),
         ],
         compiler_params=pltpu.CompilerParams(
-            collective_id=0, has_side_effects=True, vmem_limit_bytes=56 << 20
+            collective_id=0, has_side_effects=True, vmem_limit_bytes=54 << 20
         ),
-    )(slot_k, slot_src, ids, state, weights)
+    )(slot_k, slot_src, gamma, ids, coefs, land, state, weights)
+
+
+def finish_kernel(
+    gamma, state, coefs, land, recv, section, rest, halo_x, halo_y, new, recv_out, kc
+):
+    f = pl.program_id(0)
+    comp = lax.axis_index("comp")
+
+    @pl.when(f == 0)
+    def _():
+        def prepare(i, carry):
+            slopes(i, coefs, land, comp, kc)
+            return carry
+
+        lax.fori_loop(0, 16, prepare, 0)
+
+    mix_a, mix_b = mixes(comp)
+    rate_of = gamma[0, f]
+    above = halo_x[0, pl.ds(f, 1), :]
+    below = halo_x[1, pl.ds(f, 1), :]
+    mine = lax.broadcasted_iota(jnp.int32, (8, 128), 1) == f
+    for i in range(16):
+        rows = pl.ds(i * 8, 8)
+        weight = [kc[n, rows, :] for n in range(5)]
+        keep = kc[5, rows, :]
+        left = jnp.sum(jnp.where(mine, halo_y[0, rows, :], 0.0), axis=1, keepdims=True)
+        right = jnp.sum(jnp.where(mine, halo_y[1, rows, :], 0.0), axis=1, keepdims=True)
+        cur = section[0, rows, :]
+        prev = jnp.broadcast_to(above, (8, CY)) if i == 0 else section[0, i * 8 - 8 : i * 8, :]
+        nxt = (
+            jnp.broadcast_to(below, (8, CY))
+            if i == 15
+            else section[0, i * 8 + 8 : i * 8 + 16, :]
+        )
+        rate = stencil(cur, prev, nxt, left, right, weight)
+        cells = recv[0, rows, :]
+        rate = rate + (rate_of * keep) * (cells - cur)
+        new[0, 0, rows, :] = mix_a * state[0, 0, rows, :] + (1.0 - mix_a) * cur + mix_b * rate
+        new[1, 0, rows, :] = rest[0, rows, :]
+        recv_out[0, rows, :] = cells
+
+
+def finish(gamma, state, coefs, land, recv, section, rest, halo_x, halo_y):
+    field = pl.BlockSpec((1, CX, CY), lambda f: (f, 0, 0))
+    return pl.pallas_call(
+        finish_kernel,
+        grid=(CH,),
+        out_shape=[
+            jax.ShapeDtypeStruct((2, CH, CX, CY), F32),
+            jax.ShapeDtypeStruct((CH, CX, CY), F32),
+        ],
+        in_specs=[
+            pl.BlockSpec(memory_space=pltpu.SMEM),
+            pl.BlockSpec((1, 1, CX, CY), lambda f: (0, f, 0, 0)),
+            pl.BlockSpec((1, 3, CX, CY), lambda f: (0, 0, 0, 0)),
+            pl.BlockSpec((CX, CY), lambda f: (0, 0)),
+            field,
+            field,
+            field,
+            pl.BlockSpec((2, CH, CY), lambda f: (0, 0, 0)),
+            pl.BlockSpec((2, CX, 128), lambda f: (0, 0, 0)),
+        ],
+        out_specs=[pl.BlockSpec((2, 1, CX, CY), lambda f: (0, f, 0, 0)), field],
+        scratch_shapes=[pltpu.VMEM((6, CX, CY), F32)],
+        compiler_params=pltpu.CompilerParams(vmem_limit_bytes=60 << 20),
+    )(gamma, state, coefs, land, recv, section, rest, halo_x, halo_y)
 
 
 def body(state, coefs, land_sea, gamma, pair_src, pair_dev, pair_blk, weights):
-    comp_index = lax.axis_index("comp")
-    cells_x, cells_y = state.shape[2], state.shape[3]
     slot_k, slot_src, slot_id = plan(
         pair_src.reshape(PAIRS), pair_dev.reshape(PAIRS), pair_blk.reshape(PAIRS)
     )
     ids = jnp.tile(slot_id.astype(F32).reshape(TILES, 1, CAP), (1, 1, 8))
-    recv = remap(slot_k, slot_src, ids, state, weights)
-    is_atmos = comp_index == 0
-    keep = jnp.where(
-        is_atmos, jnp.ones((cells_x, cells_y), jnp.float32), land_sea.astype(jnp.float32)
-    )
-    mix_a = jnp.where(is_atmos, 0.0, 0.5).astype(jnp.float32)
-    mix_b = jnp.where(is_atmos, 1.0, 0.5).astype(jnp.float32)
-    start = state[0]
-    local_coefs = coefs[0]
-    rates = gamma[0]
-    first = tendency(shallow_rims(start), local_coefs, recv, rates, keep)
-    section = start + first
-    second = tendency(shallow_rims(section), local_coefs, recv, rates, keep)
-    result = mix_a * start + (1.0 - mix_a) * section + mix_b * second
-    return (result[None], recv[None])
+    recv, section, rest, halo_x, halo_y = remap(
+        slot_k, slot_src, gamma, ids, coefs, land_sea, state, weights
+    )
+    new, recv_out = finish(
+        gamma, state, coefs, land_sea, recv, section, rest, halo_x, halo_y
+    )
+    return (new.reshape(1, NF, CX, CY), recv_out[None])
 
 
 def solution(mesh):

time: 178 us -> 105 us (0.59)
  the two profiles are of different devices: /device:TPU:39 before, /device:TPU:9 now
where the time goes in v2:
time: 105 us
  Pallas kernels  102 us (97%)
    pallas_call x1, Pallas kernels, remap(): pl.pallas_call(remap_kernel, out_shape=[half, half, half, jax.ShapeDtypeS...  84.2 us
    pallas_call x1, Pallas kernels, finish(): pl.pallas_call(finish_kernel, grid=(CH,), out_shape=[jax.ShapeDtypeStruct...  10.5 us
    pallas_call x1, Pallas kernels, plan(): pl.pallas_call(plan_kernel, out_shape=[jax.ShapeDtypeStruct((SLOTS,), jnp...  7.56 us

profile of v2, /device:TPU:9, one launch (start us, length us, event | category | flops | bytes accessed | tf_op | source)
XLA Modules:
  0.0 104.5 jit_solution(8983660781091195168)
XLA Ops:
  0.6 7.6 %shard_map.95 = (s32[1024]{0:T(1024)}, s32[1024]{0:T(1024)}, s32[1024]{0:T(1024)}) custom-call(s32[512]{0:T(512)} %bitcast.7, s32[512]{0:T(512)} %bitcast.8, s32[512]{0:T(512)} %bitcast.9), custom_call_target="tpu_custom_call" | custom-call | tf_op jit(solution)/shard_map/pallas_call | solution.py:56
  8.2 0.7 convert_element_type.3
  8.9 0.1 tile.10
  9.0 0.1 copy.10
  9.0 0.7 copy.11.ids
  9.8 84.2 %shard_map.96 = (f32[8,128,512]{2,1,0:T(8,128)}, f32[8,128,512]{2,1,0:T(8,128)}, f32[8,128,512]{2,1,0:T(8,128)}, f32[2,8,512]{2,1,0:T(8,128)}, f32[2,128,128]{2,1,0:T(8,128)}) custom-call(s32[1024]{0:T(1024)} %get-tuple-element.12.slot_k, s32[1024]{0:T(1024)} %get-tuple-element.13.slot_src, f32[1,8]{1,0:T(1,128)} %gamma.3, f32[64,1,128]{2,1,0:T(1,128)} %copy.11.ids, ...), custom_call_target="tpu_custom_call" | custom-call | tf_op jit(solution)/shard_map/pallas_call | solution.py:435
  94.0 10.5 %shard_map.97 = (f32[2,8,128,512]{3,2,1,0:T(8,128)}, f32[8,128,512]{2,1,0:T(8,128)}) custom-call(f32[1,8]{1,0:T(1,128)} %gamma.3, f32[1,16,128,512]{3,2,1,0:T(8,128)} %state.3, f32[1,3,128,512]{3,2,1,0:T(8,128)} %coefs.3, s32[128,512]{1,0:T(8,128)} %land.3, f32[8,128,512]{2,1,0:T(8,128)} %get-tuple-element.15.recv, ...), custom_call_target="tpu_custom_call" | custom-call | tf_op jit(solution)/shard_map/pallas_call | solution.py:517
  (1 shorter events, 0.0 us)

commit v3 on v2

--- a/solution.py
+++ b/solution.py
@@ -19,47 +19,6 @@
 NF = 16
 CX = 128
 CY = 512
-
-
-def plan_kernel(src, dev, blk, slot_k, slot_src, slot_id, count):
-    def clear(i, carry):
-        slot_k[i] = 0
-        slot_src[i] = 0
-        slot_id[i] = NB
-        return carry
-
-    lax.fori_loop(0, SLOTS, clear, 0, unroll=8)
-
-    def clear_count(i, carry):
-        count[i] = 0
-        return carry
-
-    lax.fori_loop(0, TILES, clear_count, 0, unroll=8)
-
-    def place(k, carry):
-        d = dev[k]
-        r = count[d]
-        count[d] = r + 1
-        s = d * CAP + r
-        b = blk[k]
-        x = b >> 2
-        slot_k[s] = k
-        slot_src[s] = src[k]
-        slot_id[s] = (x >> 3) * 32 + (b & 3) * 8 + (x & 7)
-        return carry
-
-    lax.fori_loop(0, PAIRS, place, 0, unroll=8)
-
-
-def plan(src, dev, blk):
-    smem = pl.BlockSpec(memory_space=pltpu.SMEM)
-    return pl.pallas_call(
-        plan_kernel,
-        out_shape=[jax.ShapeDtypeStruct((SLOTS,), jnp.int32)] * 3,
-        in_specs=[smem] * 3,
-        out_specs=[smem] * 3,
-        scratch_shapes=[pltpu.SMEM((TILES,), jnp.int32)],
-    )(src, dev, blk)
 
 
 def slopes(i, coefs, land, comp, kc):
@@ -95,19 +54,23 @@
 
 
 def remap_kernel(
-    slot_k,
-    slot_src,
     gamma,
-    ids,
+    src,
+    dev,
+    blk,
+    coefs_hbm,
+    land_hbm,
+    state,
+    weights,
+    new,
+    out,
+    names_of,
+    plan,
+    table,
+    rest,
+    cells_of,
     coefs,
     land,
-    state,
-    weights,
-    out,
-    section,
-    rest,
-    halo_x,
-    halo_y,
     wbuf,
     surf,
     send,
@@ -139,10 +102,19 @@
     core = ty % 2
     sign = 1 - 2 * core
 
-    load_state = pltpu.make_async_copy(state.at[0], sp.at[:, 8 : 8 + CX, :], lsem.at[0])
-    load_state.start()
-    load = pltpu.make_async_copy(weights.at[0], wbuf, lsem.at[1])
-    load.start()
+    loads = [
+        pltpu.make_async_copy(
+            state.at[0, 0:CH], sp.at[0:CH, 8 : 8 + CX, :], lsem.at[0]
+        ),
+        pltpu.make_async_copy(weights.at[0], wbuf, lsem.at[1]),
+        pltpu.make_async_copy(
+            state.at[0, CH:NF], sp.at[CH:NF, 8 : 8 + CX, :], lsem.at[2]
+        ),
+    ]
+    loads.append(pltpu.make_async_copy(coefs_hbm, coefs, lsem.at[4]))
+    loads.append(pltpu.make_async_copy(land_hbm, land, lsem.at[5]))
+    for n in (0, 3, 4, 1, 2):
+        loads[n].start()
 
     def partner(i):
         dh = lax.rem(i, 2)
@@ -162,21 +134,54 @@
 
     barrier = pltpu.get_barrier_semaphore()
 
-    def greet(i, carry):
-        to_x, to_y = partner(i)
-        pl.semaphore_signal(barrier, 1, device_id=(1 - comp, to_x, to_y), device_id_type=MESH)
-        return carry
-
-    lax.fori_loop(0, TILES, greet, 0)
     for to in beside:
         pl.semaphore_signal(barrier, 1, device_id=to, device_id_type=MESH)
 
     def prepare(i, carry):
+        for j in range(4):
+            to_x, to_y = partner(i * 4 + j)
+            pl.semaphore_signal(barrier, 1, device_id=(1 - comp, to_x, to_y), device_id_type=MESH)
         slopes(i, coefs, land, comp, kc)
         return carry
 
+    loads[3].wait()
+    loads[4].wait()
     lax.fori_loop(0, 16, prepare, 0)
-    load_state.wait()
+
+    target = dev[...]
+    member = lax.broadcasted_iota(jnp.int32, (TILES, PAIRS), 0) == target
+    one_of = jnp.where(member, 1.0, 0.0).astype(BF16)
+    before = jnp.where(
+        lax.broadcasted_iota(jnp.int32, (PAIRS, PAIRS), 0)
+        < lax.broadcasted_iota(jnp.int32, (PAIRS, PAIRS), 1),
+        1.0,
+        0.0,
+    ).astype(BF16)
+    counted = jnp.dot(one_of, before, preferred_element_type=F32)
+    rank = jnp.sum(jnp.where(member, counted, 0.0), axis=0, keepdims=True)
+    at_rank = lax.broadcasted_iota(jnp.int32, (128, PAIRS), 0) % CAP
+    at_rank = jnp.where(at_rank.astype(F32) == rank, 1.0, 0.0).astype(BF16)
+    number = lax.broadcasted_iota(jnp.int32, (1, PAIRS), 1)
+    b = blk[...]
+    b = (b // 32) * 32 + (b % 4) * 8 + (b // 4) % 8
+
+    def tabled(value):
+        rows = jnp.where(member, value.astype(F32), 0.0).astype(BF16)
+        return lax.dot_general(
+            rows, at_rank, (((1,), (1,)), ((), ())), preferred_element_type=F32
+        )
+
+    def placed(value):
+        return 2.0 * tabled(value // 2) + tabled(value % 2)
+
+    table[0] = placed(number).astype(jnp.int32)
+    table[1] = placed(src[...]).astype(jnp.int32)
+    to_smem = pltpu.make_async_copy(table, plan, lsem.at[3])
+    to_smem.start()
+    names = placed(b) + float(NB) * (1.0 - tabled(jnp.ones((1, PAIRS), jnp.int32)))
+    for d in range(TILES):
+        names_of[d] = names[d : d + 1, :]
+    loads[0].wait()
 
     def relay(i, carry):
         for yb in range(4):
@@ -230,20 +235,6 @@
         for n, (place, end) in enumerate(((ty, 0), (ty, 7))):
             yr[e, n] = jnp.where(place == end, 0.0, yr[e, n])
 
-    def pack_state(i, carry):
-        rows = pl.ds(pl.multiple_of(i * 8 + 8, 8), 8)
-        pack_columns(0, i, [sp[f, rows, :] for f in range(NF)])
-        return carry
-
-    lax.fori_loop(0, 16, pack_state, 0)
-    for f in range(NF):
-        xs[0, 0, f : f + 1, :] = sp[f, 7 + CX : 8 + CX, :]
-        xs[0, 1, f : f + 1, :] = sp[f, 8:9, :]
-
-    pl.semaphore_wait(barrier, TILES + 4)
-    for move in edges(0):
-        move.start()
-
     def copies(i):
         to_x, to_y = partner(i)
         to = (1 - comp, to_x, to_y)
@@ -251,7 +242,7 @@
             send.at[i], recv.at[i], ssem.at[i], rsem.at[i], device_id=to, device_id_type=MESH
         )
         names = pltpu.make_async_remote_copy(
-            ids.at[to_x * 8 + to_y],
+            names_of.at[to_x * 8 + to_y],
             recv_ids.at[i],
             isend.at[i],
             irecv.at[i],
@@ -260,7 +251,9 @@
         )
         return data, names, to_x * 8 + to_y
 
-    load.wait()
+    to_smem.wait()
+    loads[1].wait()
+    pl.semaphore_wait(barrier, TILES + 4)
 
     def produce(i, carry):
         data, names, tile = copies(i)
@@ -270,9 +263,8 @@
             ws = []
             ps = []
             for j in range(4):
-                s = tile * CAP + g * 4 + j
-                ws.append(wbuf[slot_k[s]])
-                ps.append(surf[slot_src[s]])
+                ws.append(wbuf[jnp.clip(plan[0, tile, g * 4 + j], 0, PAIRS - 1)])
+                ps.append(surf[jnp.clip(plan[1, tile, g * 4 + j], 0, NB - 1)])
             lhs = jnp.concatenate(
                 [
                     jnp.concatenate([ps[0], zero, ps[2], zero], axis=0),
@@ -296,7 +288,23 @@
         data.start()
         return carry
 
-    lax.fori_loop(0, TILES, produce, 0)
+    lax.fori_loop(0, 8, produce, 0)
+    loads[2].wait()
+
+    def pack_state(i, carry):
+        rows = pl.ds(pl.multiple_of(i * 8 + 8, 8), 8)
+        pack_columns(0, i, [sp[f, rows, :] for f in range(NF)])
+        return carry
+
+    lax.fori_loop(0, 16, pack_state, 0)
+    for f in range(NF):
+        xs[0, 0, f : f + 1, :] = sp[f, 7 + CX : 8 + CX, :]
+        xs[0, 1, f : f + 1, :] = sp[f, 8:9, :]
+
+    for move in edges(0):
+        move.start()
+
+    lax.fori_loop(8, 40, produce, 0)
 
     mix_a, mix_b = mixes(comp)
     settle(0)
@@ -331,6 +339,7 @@
         xs[1, 1, f : f + 1, :] = sq[f, 8:9, :]
     for move in edges(1):
         move.start()
+    lax.fori_loop(40, TILES, produce, 0)
     settle(1)
     for f in range(CH):
         sq[f, 7:8, :] = xr[1, 0, f : f + 1, :]
@@ -348,6 +357,8 @@
         return carry
 
     lax.fori_loop(0, 16, second_step, 0)
+    stores = [pltpu.make_async_copy(rest, new.at[0, CH:NF], lsem.at[0])]
+    stores[0].start()
 
     def arrive(i, carry):
         data, names, _ = copies(i)
@@ -397,19 +408,21 @@
                 [acc[f, pl.ds(pl.multiple_of(i * 32 + yb * 8, 8), 8), :] for yb in range(4)],
                 axis=1,
             )
-            out[f, rows, :] = cells
+            cells_of[f, rows, :] = cells
             moved = part[f, rows, :] + (gamma[0, f] * keep) * cells
-            section[f, rows, :] = moved
+            sq[f, pl.ds(pl.multiple_of(i * 8 + 8, 8), 8), :] = moved
             strips.append(moved)
         pack_columns(2, i, strips)
         return carry
 
     lax.fori_loop(0, 16, couple, 0)
     for f in range(CH):
-        xs[2, 0, f : f + 1, :] = section[f, CX - 1 : CX, :]
-        xs[2, 1, f : f + 1, :] = section[f, 0:1, :]
+        xs[2, 0, f : f + 1, :] = sq[f, 7 + CX : 8 + CX, :]
+        xs[2, 1, f : f + 1, :] = sq[f, 8:9, :]
     for move in edges(2):
         move.start()
+    stores.append(pltpu.make_async_copy(cells_of, out.at[0], lsem.at[1]))
+    stores[1].start()
 
     def sent(i, carry):
         data, names, _ = copies(i)
@@ -419,31 +432,58 @@
 
     lax.fori_loop(0, TILES, sent, 0)
     settle(2)
-    for n in range(2):
-        halo_x[n] = xr[2, n, 0:CH, :]
-        halo_y[n] = yr[2, n]
+    for f in range(CH):
+        sq[f, 7:8, :] = xr[2, 0, f : f + 1, :]
+        sq[f, 8 + CX : 9 + CX, :] = xr[2, 1, f : f + 1, :]
+
+    def last_step(i, carry):
+        rows = pl.ds(pl.multiple_of(i * 8, 8), 8)
+        weight = [kc[n, rows, :] for n in range(5)]
+        keep = kc[5, rows, :]
+        left, right = yr[2, 0, rows, :], yr[2, 1, rows, :]
+        for f in range(CH):
+            cur, prev, nxt = around(sq, f, i)
+            rate = stencil(cur, prev, nxt, left[:, f : f + 1], right[:, f : f + 1], weight)
+            rate = rate + (gamma[0, f] * keep) * (cells_of[f, rows, :] - cur)
+            start = sp[f, pl.ds(pl.multiple_of(i * 8 + 8, 8), 8), :]
+            part[f, rows, :] = mix_a * start + (1.0 - mix_a) * cur + mix_b * rate
+        return carry
+
+    for q in range(4):
+        lax.fori_loop(4 * q, 4 * q + 4, last_step, 0)
+        rows = pl.ds(32 * q, 32)
+        store = pltpu.make_async_copy(
+            part.at[:, rows, :], new.at[0, 0:CH, rows, :], lsem.at[2 + q]
+        )
+        store.start()
+        stores.append(store)
     for e in range(3):
         for move in edges(e):
             move.wait_send()
-
-
-def remap(slot_k, slot_src, gamma, ids, coefs, land, state, weights):
+    for store in stores:
+        store.wait()
+
+
+def remap(gamma, src, dev, blk, coefs, land, state, weights):
     smem = pl.BlockSpec(memory_space=pltpu.SMEM)
     vmem = pl.BlockSpec(memory_space=pltpu.VMEM)
     hbm = pl.BlockSpec(memory_space=pl.ANY)
-    half = jax.ShapeDtypeStruct((CH, CX, CY), F32)
     return pl.pallas_call(
         remap_kernel,
         out_shape=[
-            half,
-            half,
-            half,
-            jax.ShapeDtypeStruct((2, CH, CY), F32),
-            jax.ShapeDtypeStruct((2, CX, 128), F32),
+            jax.ShapeDtypeStruct((1, NF, CX, CY), F32),
+            jax.ShapeDtypeStruct((1, CH, CX, CY), F32),
         ],
-        in_specs=[smem, smem, smem, vmem, vmem, vmem, hbm, hbm],
-        out_specs=[vmem] * 5,
+        in_specs=[smem, vmem, vmem, vmem, hbm, hbm, hbm, hbm],
+        out_specs=[hbm] * 2,
         scratch_shapes=[
+            pltpu.VMEM((TILES, 1, 128), F32),
+            pltpu.SMEM((2, TILES, 128), jnp.int32),
+            pltpu.VMEM((2, TILES, 128), jnp.int32),
+            pltpu.VMEM((CH, CX, CY), F32),
+            pltpu.VMEM((CH, CX, CY), F32),
+            pltpu.VMEM((1, 3, CX, CY), F32),
+            pltpu.VMEM((CX, CY), jnp.int32),
             pltpu.VMEM((PAIRS, 128, 128), BF16),
             pltpu.VMEM((NB, CH, 128), F32),
             pltpu.VMEM((TILES, CH * CAP, 128), F32),
@@ -458,7 +498,7 @@
             pltpu.VMEM((3, 2, NF, CY), F32),
             pltpu.VMEM((3, 2, CX, 128), F32),
             pltpu.VMEM((3, 2, CX, 128), F32),
-            pltpu.SemaphoreType.DMA((2,)),
+            pltpu.SemaphoreType.DMA((6,)),
             pltpu.SemaphoreType.DMA((TILES,)),
             pltpu.SemaphoreType.DMA((TILES,)),
             pltpu.SemaphoreType.DMA((TILES,)),
@@ -467,89 +507,22 @@
             pltpu.SemaphoreType.DMA((3, 4)),
         ],
         compiler_params=pltpu.CompilerParams(
-            collective_id=0, has_side_effects=True, vmem_limit_bytes=54 << 20
+            collective_id=0, has_side_effects=True, vmem_limit_bytes=56 << 20
         ),
-    )(slot_k, slot_src, gamma, ids, coefs, land, state, weights)
-
-
-def finish_kernel(
-    gamma, state, coefs, land, recv, section, rest, halo_x, halo_y, new, recv_out, kc
-):
-    f = pl.program_id(0)
-    comp = lax.axis_index("comp")
-
-    @pl.when(f == 0)
-    def _():
-        def prepare(i, carry):
-            slopes(i, coefs, land, comp, kc)
-            return carry
-
-        lax.fori_loop(0, 16, prepare, 0)
-
-    mix_a, mix_b = mixes(comp)
-    rate_of = gamma[0, f]
-    above = halo_x[0, pl.ds(f, 1), :]
-    below = halo_x[1, pl.ds(f, 1), :]
-    mine = lax.broadcasted_iota(jnp.int32, (8, 128), 1) == f
-    for i in range(16):
-        rows = pl.ds(i * 8, 8)
-        weight = [kc[n, rows, :] for n in range(5)]
-        keep = kc[5, rows, :]
-        left = jnp.sum(jnp.where(mine, halo_y[0, rows, :], 0.0), axis=1, keepdims=True)
-        right = jnp.sum(jnp.where(mine, halo_y[1, rows, :], 0.0), axis=1, keepdims=True)
-        cur = section[0, rows, :]
-        prev = jnp.broadcast_to(above, (8, CY)) if i == 0 else section[0, i * 8 - 8 : i * 8, :]
-        nxt = (
-            jnp.broadcast_to(below, (8, CY))
-            if i == 15
-            else section[0, i * 8 + 8 : i * 8 + 16, :]
-        )
-        rate = stencil(cur, prev, nxt, left, right, weight)
-        cells = recv[0, rows, :]
-        rate = rate + (rate_of * keep) * (cells - cur)
-        new[0, 0, rows, :] = mix_a * state[0, 0, rows, :] + (1.0 - mix_a) * cur + mix_b * rate
-        new[1, 0, rows, :] = rest[0, rows, :]
-        recv_out[0, rows, :] = cells
-
-
-def finish(gamma, state, coefs, land, recv, section, rest, halo_x, halo_y):
-    field = pl.BlockSpec((1, CX, CY), lambda f: (f, 0, 0))
-    return pl.pallas_call(
-        finish_kernel,
-        grid=(CH,),
-        out_shape=[
-            jax.ShapeDtypeStruct((2, CH, CX, CY), F32),
-            jax.ShapeDtypeStruct((CH, CX, CY), F32),
-        ],
-        in_specs=[
-            pl.BlockSpec(memory_space=pltpu.SMEM),
-            pl.BlockSpec((1, 1, CX, CY), lambda f: (0, f, 0, 0)),
-            pl.BlockSpec((1, 3, CX, CY), lambda f: (0, 0, 0, 0)),
-            pl.BlockSpec((CX, CY), lambda f: (0, 0)),
-            field,
-            field,
-            field,
-            pl.BlockSpec((2, CH, CY), lambda f: (0, 0, 0)),
-            pl.BlockSpec((2, CX, 128), lambda f: (0, 0, 0)),
-        ],
-        out_specs=[pl.BlockSpec((2, 1, CX, CY), lambda f: (0, f, 0, 0)), field],
-        scratch_shapes=[pltpu.VMEM((6, CX, CY), F32)],
-        compiler_params=pltpu.CompilerParams(vmem_limit_bytes=60 << 20),
-    )(gamma, state, coefs, land, recv, section, rest, halo_x, halo_y)
+    )(gamma, src, dev, blk, coefs, land, state, weights)
 
 
 def body(state, coefs, land_sea, gamma, pair_src, pair_dev, pair_blk, weights):
-    slot_k, slot_src, slot_id = plan(
-        pair_src.reshape(PAIRS), pair_dev.reshape(PAIRS), pair_blk.reshape(PAIRS)
+    return remap(
+        gamma,
+        pair_src,
+        pair_dev.reshape(1, PAIRS),
+        pair_blk,
+        coefs,
+        land_sea,
+        state,
+        weights,
     )
-    ids = jnp.tile(slot_id.astype(F32).reshape(TILES, 1, CAP), (1, 1, 8))
-    recv, section, rest, halo_x, halo_y = remap(
-        slot_k, slot_src, gamma, ids, coefs, land_sea, state, weights
-    )
-    new, recv_out = finish(
-        gamma, state, coefs, land_sea, recv, section, rest, halo_x, halo_y
-    )
-    return (new.reshape(1, NF, CX, CY), recv_out[None])
 
 
 def solution(mesh):

time: 105 us -> 86.7 us (0.83)
  the two profiles are of different devices: /device:TPU:9 before, /device:TPU:40 now
where the time goes in v3:
time: 86.7 us; the launch traced here: 86.5 us
  Pallas kernels  79.6 us (92%)
  local copies, waits for them, and re-layouts  6.28 us (7%)
    pallas_call x1, Pallas kernels, remap(): pl.pallas_call(remap_kernel, out_shape=[jax.ShapeDtypeStruct((1, NF, CX,...  79.6 us
    unnamed x4, local copies, waits for them, and re-layouts  6.28 us

profile of v3, /device:TPU:40, one launch (start us, length us, event | category | flops | bytes accessed | tf_op | source)
XLA Modules:
  0.0 86.5 jit_solution(7261964069665010103)
XLA Ops:
  0.6 79.6 %shard_map.95 = (f32[1,16,128,512]{3,2,1,0:T(8,128)}, f32[1,8,128,512]{3,2,1,0:T(8,128)}) custom-call(f32[1,8]{1,0:T(1,128)} %gamma.1, s32[1,512]{1,0:T(1,128)} %src.1, s32[1,512]{1,0:T(1,128)} %bitcast.1, s32[1,512]{1,0:T(1,128)} %blk.1, f32[1,3,128,512]{3,2,1,0:T(8,128)} %coefs_hbm.1, s32[128,512]{1,0:T(8,128)} %land_hbm.1, f32[1,16,128,512]{3,2,1,0:T(8,128)} %state.1, ...), custom_call_target="tpu_custom_call" | custom-call | tf_op jit(solution)/shard_map/pallas_call | solution.py:471
  80.2 0.0 copy-start
  80.2 5.0 %copy.12 = f32[1,16,128,512]{3,2,1,0:T(8,128)} copy(f32[1,16,128,512]{3,2,1,0:T(8,128)} %get-tuple-element.4) | data formatting | bytes 8388608
  85.2 0.0 copy-done
  85.2 1.3 %copy.13 = f32[1,8,128,512]{3,2,1,0:T(8,128)} copy(f32[1,8,128,512]{3,2,1,0:T(8,128)S(1)} %copy-done) | data formatting | bytes 4194304
Async XLA Ops:
  80.2 5.0 %copy-start = (f32[1,8,128,512]{3,2,1,0:T(8,128)S(1)}, f32[1,8,128,512]{3,2,1,0:T(8,128)}, u32[]{:S(2)}) copy-start(f32[1,8,128,512]{3,2,1,0:T(8,128)} %get-tuple-element.5) | copy-start | bytes 6291460

commit v4 on v3

--- a/solution.py
+++ b/solution.py
@@ -21,18 +21,19 @@
 CY = 512
 
 
-def slopes(i, coefs, land, comp, kc):
-    rows = pl.ds(pl.multiple_of(i * 8, 8), 8)
+def slopes(rows, coefs, land, comp):
     u = coefs[0, 0, rows, :]
     v = coefs[0, 1, rows, :]
     kappa = coefs[0, 2, rows, :]
     keep = jnp.where(comp == 0, 1.0, land[rows, :].astype(F32))
-    kc[0, rows, :] = keep * (jnp.maximum(u, 0.0) + kappa)
-    kc[1, rows, :] = keep * (kappa - jnp.minimum(u, 0.0))
-    kc[2, rows, :] = keep * (jnp.maximum(v, 0.0) + kappa)
-    kc[3, rows, :] = keep * (kappa - jnp.minimum(v, 0.0))
-    kc[4, rows, :] = -keep * (jnp.abs(u) + jnp.abs(v) + 4.0 * kappa)
-    kc[5, rows, :] = keep
+    return [
+        keep * (jnp.maximum(u, 0.0) + kappa),
+        keep * (kappa - jnp.minimum(u, 0.0)),
+        keep * (jnp.maximum(v, 0.0) + kappa),
+        keep * (kappa - jnp.minimum(v, 0.0)),
+        -keep * (jnp.abs(u) + jnp.abs(v) + 4.0 * kappa),
+        keep,
+    ]
 
 
 def stencil(cur, prev, nxt, left, right, weight):
@@ -62,8 +63,11 @@
     land_hbm,
     state,
     weights,
-    new,
     out,
+    section,
+    others,
+    halo_x,
+    halo_y,
     names_of,
     plan,
     table,
@@ -113,7 +117,7 @@
     ]
     loads.append(pltpu.make_async_copy(coefs_hbm, coefs, lsem.at[4]))
     loads.append(pltpu.make_async_copy(land_hbm, land, lsem.at[5]))
-    for n in (0, 3, 4, 1, 2):
+    for n in (0, 1, 3, 4, 2):
         loads[n].start()
 
     def partner(i):
@@ -137,16 +141,15 @@
     for to in beside:
         pl.semaphore_signal(barrier, 1, device_id=to, device_id_type=MESH)
 
-    def prepare(i, carry):
-        for j in range(4):
-            to_x, to_y = partner(i * 4 + j)
+    to_xs = [
+        lax.rem(h + dh, 2) * 4 + lax.rem(x + sign * dx + 4, 4) for dh in range(2) for dx in range(4)
+    ]
+    to_ys = [
+        lax.rem(y + sign * dy + 4, 4) * 2 + lax.rem(core + dc, 2) for dy in range(4) for dc in range(2)
+    ]
+    for to_x in to_xs:
+        for to_y in to_ys:
             pl.semaphore_signal(barrier, 1, device_id=(1 - comp, to_x, to_y), device_id_type=MESH)
-        slopes(i, coefs, land, comp, kc)
-        return carry
-
-    loads[3].wait()
-    loads[4].wait()
-    lax.fori_loop(0, 16, prepare, 0)
 
     target = dev[...]
     member = lax.broadcasted_iota(jnp.int32, (TILES, PAIRS), 0) == target
@@ -291,6 +294,16 @@
     lax.fori_loop(0, 8, produce, 0)
     loads[2].wait()
 
+    def prepare(i, carry):
+        rows = pl.ds(pl.multiple_of(i * 8, 8), 8)
+        for n, value in enumerate(slopes(rows, coefs, land, comp)):
+            kc[n, rows, :] = value
+        return carry
+
+    loads[3].wait()
+    loads[4].wait()
+    lax.fori_loop(0, 16, prepare, 0)
+
     def pack_state(i, carry):
         rows = pl.ds(pl.multiple_of(i * 8 + 8, 8), 8)
         pack_columns(0, i, [sp[f, rows, :] for f in range(NF)])
@@ -357,7 +370,7 @@
         return carry
 
     lax.fori_loop(0, 16, second_step, 0)
-    stores = [pltpu.make_async_copy(rest, new.at[0, CH:NF], lsem.at[0])]
+    stores = [pltpu.make_async_copy(rest, others, lsem.at[0])]
     stores[0].start()
 
     def arrive(i, carry):
@@ -421,8 +434,12 @@
         xs[2, 1, f : f + 1, :] = sq[f, 8:9, :]
     for move in edges(2):
         move.start()
-    stores.append(pltpu.make_async_copy(cells_of, out.at[0], lsem.at[1]))
-    stores[1].start()
+    stores.append(
+        pltpu.make_async_copy(sq.at[:, 8 : 8 + CX, :], section, lsem.at[2])
+    )
+    stores.append(pltpu.make_async_copy(cells_of, out, lsem.at[1]))
+    for store in stores[1:]:
+        store.start()
 
     def sent(i, carry):
         data, names, _ = copies(i)
@@ -432,31 +449,12 @@
 
     lax.fori_loop(0, TILES, sent, 0)
     settle(2)
-    for f in range(CH):
-        sq[f, 7:8, :] = xr[2, 0, f : f + 1, :]
-        sq[f, 8 + CX : 9 + CX, :] = xr[2, 1, f : f + 1, :]
-
-    def last_step(i, carry):
-        rows = pl.ds(pl.multiple_of(i * 8, 8), 8)
-        weight = [kc[n, rows, :] for n in range(5)]
-        keep = kc[5, rows, :]
-        left, right = yr[2, 0, rows, :], yr[2, 1, rows, :]
-        for f in range(CH):
-            cur, prev, nxt = around(sq, f, i)
-            rate = stencil(cur, prev, nxt, left[:, f : f + 1], right[:, f : f + 1], weight)
-            rate = rate + (gamma[0, f] * keep) * (cells_of[f, rows, :] - cur)
-            start = sp[f, pl.ds(pl.multiple_of(i * 8 + 8, 8), 8), :]
-            part[f, rows, :] = mix_a * start + (1.0 - mix_a) * cur + mix_b * rate
-        return carry
-
-    for q in range(4):
-        lax.fori_loop(4 * q, 4 * q + 4, last_step, 0)
-        rows = pl.ds(32 * q, 32)
-        store = pltpu.make_async_copy(
-            part.at[:, rows, :], new.at[0, 0:CH, rows, :], lsem.at[2 + q]
-        )
-        store.start()
-        stores.append(store)
+    for copy in (
+        pltpu.make_async_copy(xr.at[2, :, 0:CH, :], halo_x, lsem.at[3]),
+        pltpu.make_async_copy(yr.at[2], halo_y, lsem.at[4]),
+    ):
+        copy.start()
+        stores.append(copy)
     for e in range(3):
         for move in edges(e):
             move.wait_send()
@@ -468,14 +466,18 @@
     smem = pl.BlockSpec(memory_space=pltpu.SMEM)
     vmem = pl.BlockSpec(memory_space=pltpu.VMEM)
     hbm = pl.BlockSpec(memory_space=pl.ANY)
+    half = jax.ShapeDtypeStruct((CH, CX, CY), F32)
     return pl.pallas_call(
         remap_kernel,
         out_shape=[
-            jax.ShapeDtypeStruct((1, NF, CX, CY), F32),
-            jax.ShapeDtypeStruct((1, CH, CX, CY), F32),
+            half,
+            half,
+            half,
+            jax.ShapeDtypeStruct((2, CH, CY), F32),
+            jax.ShapeDtypeStruct((2, CX, 128), F32),
         ],
         in_specs=[smem, vmem, vmem, vmem, hbm, hbm, hbm, hbm],
-        out_specs=[hbm] * 2,
+        out_specs=[hbm] * 5,
         scratch_shapes=[
             pltpu.VMEM((TILES, 1, 128), F32),
             pltpu.SMEM((2, TILES, 128), jnp.int32),
@@ -512,8 +514,141 @@
     )(gamma, src, dev, blk, coefs, land, state, weights)
 
 
+PARTS = 4
+
+
+def finish_kernel(
+    gamma,
+    state,
+    coefs_hbm,
+    land_hbm,
+    recv,
+    section,
+    others,
+    halo_x_hbm,
+    halo_y_hbm,
+    new,
+    recv_out,
+    cells_of,
+    around_of,
+    start_of,
+    done,
+    coefs,
+    land,
+    halo_x,
+    halo_y,
+    rest,
+    csem,
+    lsem,
+    ssem,
+):
+    comp = lax.axis_index("comp")
+    mix_a, mix_b = mixes(comp)
+    depth = CX // PARTS
+    common = [
+        pltpu.make_async_copy(halo_x_hbm, halo_x, csem.at[0]),
+        pltpu.make_async_copy(halo_y_hbm, halo_y, csem.at[1]),
+    ]
+    loads = []
+    for q in range(PARTS):
+        rows = pl.ds(q * depth, depth)
+        inner = pl.ds(8 + q * depth, depth)
+        loads.append(
+            [
+                pltpu.make_async_copy(section.at[:, rows, :], around_of.at[:, inner, :], lsem.at[q, 0]),
+                pltpu.make_async_copy(coefs_hbm.at[:, :, rows, :], coefs.at[:, :, rows, :], lsem.at[q, 1]),
+                pltpu.make_async_copy(land_hbm.at[rows, :], land.at[rows, :], lsem.at[q, 2]),
+                pltpu.make_async_copy(recv.at[:, rows, :], cells_of.at[:, rows, :], lsem.at[q, 3]),
+                pltpu.make_async_copy(state.at[0, 0:CH, rows, :], start_of.at[:, rows, :], lsem.at[q, 4]),
+            ]
+        )
+    kept = pltpu.make_async_copy(others, rest, csem.at[2])
+    loads[0][0].start()
+    for load in common:
+        load.start()
+    for load in loads[0][1:]:
+        load.start()
+    for q in range(1, PARTS):
+        for load in loads[q]:
+            load.start()
+    kept.start()
+
+    for load in common:
+        load.wait()
+    loads[0][0].wait()
+    for f in range(CH):
+        around_of[f, 7:8, :] = halo_x[0, f : f + 1, :]
+        around_of[f, 8 + CX : 9 + CX, :] = halo_x[1, f : f + 1, :]
+
+    stores = []
+    for q in range(PARTS):
+        if q + 1 < PARTS:
+            loads[q + 1][0].wait()
+        for load in loads[q][1:]:
+            load.wait()
+
+        def step(i, carry):
+            rows = pl.ds(pl.multiple_of(i * 8, 8), 8)
+            weight = slopes(rows, coefs, land, comp)
+            left, right = halo_y[0, rows, :], halo_y[1, rows, :]
+            for f in range(CH):
+                cur, prev, nxt = [
+                    around_of[f, pl.ds(pl.multiple_of(i * 8 + o, 8), 8), :] for o in (8, 0, 16)
+                ]
+                rate = stencil(cur, prev, nxt, left[:, f : f + 1], right[:, f : f + 1], weight)
+                rate = rate + (gamma[0, f] * weight[5]) * (cells_of[f, rows, :] - cur)
+                start = start_of[f, rows, :]
+                done[f, rows, :] = mix_a * start + (1.0 - mix_a) * cur + mix_b * rate
+            return carry
+
+        rows = pl.ds(q * depth, depth)
+        stores.append(
+            pltpu.make_async_copy(cells_of.at[:, rows, :], recv_out.at[0, :, rows, :], ssem.at[q, 0])
+        )
+        stores[-1].start()
+        lax.fori_loop(q * (depth // 8), (q + 1) * (depth // 8), step, 0)
+        stores.append(
+            pltpu.make_async_copy(done.at[:, rows, :], new.at[0, 0:CH, rows, :], ssem.at[q, 1])
+        )
+        stores[-1].start()
+    kept.wait()
+    stores.append(pltpu.make_async_copy(rest, new.at[0, CH:NF], csem.at[3]))
+    stores[-1].start()
+    for store in stores:
+        store.wait()
+
+
+def finish(gamma, state, coefs, land, recv, section, others, halo_x, halo_y):
+    hbm = pl.BlockSpec(memory_space=pl.ANY)
+    half = pltpu.VMEM((CH, CX, CY), F32)
+    return pl.pallas_call(
+        finish_kernel,
+        out_shape=[
+            jax.ShapeDtypeStruct((1, NF, CX, CY), F32),
+            jax.ShapeDtypeStruct((1, CH, CX, CY), F32),
+        ],
+        in_specs=[pl.BlockSpec(memory_space=pltpu.SMEM)] + [hbm] * 8,
+        out_specs=[hbm] * 2,
+        scratch_shapes=[
+            half,
+            pltpu.VMEM((CH, CX + 16, CY), F32),
+            half,
+            half,
+            pltpu.VMEM((1, 3, CX, CY), F32),
+            pltpu.VMEM((CX, CY), jnp.int32),
+            pltpu.VMEM((2, CH, CY), F32),
+            pltpu.VMEM((2, CX, 128), F32),
+            half,
+            pltpu.SemaphoreType.DMA((4,)),
+            pltpu.SemaphoreType.DMA((PARTS, 5)),
+            pltpu.SemaphoreType.DMA((PARTS, 2)),
+        ],
+        compiler_params=pltpu.CompilerParams(vmem_limit_bytes=60 << 20),
+    )(gamma, state, coefs, land, recv, section, others, halo_x, halo_y)
+
+
 def body(state, coefs, land_sea, gamma, pair_src, pair_dev, pair_blk, weights):
-    return remap(
+    recv, section, others, halo_x, halo_y = remap(
         gamma,
         pair_src,
         pair_dev.reshape(1, PAIRS),
@@ -523,6 +658,10 @@
         state,
         weights,
     )
+    new, recv_out = finish(
+        gamma, state, coefs, land_sea, recv, section, others, halo_x, halo_y
+    )
+    return new, recv_out
 
 
 def solution(mesh):

time: 86.7 us -> 84.6 us (0.976)
  the two profiles are of different devices: /device:TPU:40 before, /device:TPU:9 now
where the time goes in v4:
time: 84.6 us; the launch traced here: 83.4 us
  Pallas kernels  82.8 us (98%)
    pallas_call x1, Pallas kernels, remap(): pl.pallas_call(remap_kernel, out_shape=[half, half, half, jax.ShapeDtypeS...  74.6 us
    pallas_call x1, Pallas kernels, finish(): pl.pallas_call(finish_kernel, out_shape=[jax.ShapeDtypeStruct((1, NF, CX,...  8.17 us

profile of v4, /device:TPU:9, one launch (start us, length us, event | category | flops | bytes accessed | tf_op | source)
XLA Modules:
  0.0 83.4 jit_solution(8792713116160674152)
XLA Ops:
  0.6 74.6 %shard_map.95 = (f32[8,128,512]{2,1,0:T(8,128)}, f32[8,128,512]{2,1,0:T(8,128)}, f32[8,128,512]{2,1,0:T(8,128)}, f32[2,8,512]{2,1,0:T(8,128)}, f32[2,128,128]{2,1,0:T(8,128)}) custom-call(f32[1,8]{1,0:T(1,128)} %gamma.3, s32[1,512]{1,0:T(1,128)} %src.1, s32[1,512]{1,0:T(1,128)} %bitcast.1, s32[1,512]{1,0:T(1,128)} %blk.1, f32[1,3,128,512]{3,2,1,0:T(8,128)} %coefs_hbm.3, ...), custom_call_target="tpu_custom_call" | custom-call | tf_op jit(solution)/shard_map/pallas_call | solution.py:470
  75.3 8.2 %shard_map.96 = (f32[1,16,128,512]{3,2,1,0:T(8,128)}, f32[1,8,128,512]{3,2,1,0:T(8,128)}) custom-call(f32[1,8]{1,0:T(1,128)} %gamma.3, f32[1,16,128,512]{3,2,1,0:T(8,128)} %state.3, f32[1,3,128,512]{3,2,1,0:T(8,128)} %coefs_hbm.3, s32[128,512]{1,0:T(8,128)} %land_hbm.3, f32[8,128,512]{2,1,0:T(8,128)} %get-tuple-element.7.recv, ...), custom_call_target="tpu_custom_call" | custom-call | tf_op jit(solution)/shard_map/pallas_call | solution.py:624

commit v5 on v4

--- a/solution.py
+++ b/solution.py
@@ -447,7 +447,6 @@
         data.wait_send()
         return carry
 
-    lax.fori_loop(0, TILES, sent, 0)
     settle(2)
     for copy in (
         pltpu.make_async_copy(xr.at[2, :, 0:CH, :], halo_x, lsem.at[3]),
@@ -455,6 +454,7 @@
     ):
         copy.start()
         stores.append(copy)
+    lax.fori_loop(0, TILES, sent, 0)
     for e in range(3):
         for move in edges(e):
             move.wait_send()
@@ -514,7 +514,7 @@
     )(gamma, src, dev, blk, coefs, land, state, weights)
 
 
-PARTS = 4
+PARTS = 2
 
 
 def finish_kernel(

time: 84.6 us -> 84.4 us (level)
  no operation moved by 1% of the time
where the time goes in v5:
time: 84.4 us; the launch traced here: 83.2 us
  Pallas kernels  82.5 us (98%)
    pallas_call x1, Pallas kernels, remap(): pl.pallas_call(remap_kernel, out_shape=[half, half, half, jax.ShapeDtypeS...  74.6 us
    pallas_call x1, Pallas kernels, finish(): pl.pallas_call(finish_kernel, out_shape=[jax.ShapeDtypeStruct((1, NF, CX,...  7.89 us

profile of v5, /device:TPU:9, one launch (start us, length us, event | category | flops | bytes accessed | tf_op | source)
XLA Modules:
  0.0 83.2 jit_solution(6359883723070277112)
XLA Ops:
  0.6 74.6 %shard_map.95 = (f32[8,128,512]{2,1,0:T(8,128)}, f32[8,128,512]{2,1,0:T(8,128)}, f32[8,128,512]{2,1,0:T(8,128)}, f32[2,8,512]{2,1,0:T(8,128)}, f32[2,128,128]{2,1,0:T(8,128)}) custom-call(f32[1,8]{1,0:T(1,128)} %gamma.3, s32[1,512]{1,0:T(1,128)} %src.1, s32[1,512]{1,0:T(1,128)} %bitcast.1, s32[1,512]{1,0:T(1,128)} %blk.1, f32[1,3,128,512]{3,2,1,0:T(8,128)} %coefs_hbm.3, ...), custom_call_target="tpu_custom_call" | custom-call | tf_op jit(solution)/shard_map/pallas_call | solution.py:470
  75.3 7.9 %shard_map.96 = (f32[1,16,128,512]{3,2,1,0:T(8,128)}, f32[1,8,128,512]{3,2,1,0:T(8,128)}) custom-call(f32[1,8]{1,0:T(1,128)} %gamma.3, f32[1,16,128,512]{3,2,1,0:T(8,128)} %state.3, f32[1,3,128,512]{3,2,1,0:T(8,128)} %coefs_hbm.3, s32[128,512]{1,0:T(8,128)} %land_hbm.3, f32[8,128,512]{2,1,0:T(8,128)} %get-tuple-element.7.recv, ...), custom_call_target="tpu_custom_call" | custom-call | tf_op jit(solution)/shard_map/pallas_call | solution.py:624
